TPU v7x, 256 devices: a whole 4x4x8 slice. The times are simulated.
256 devices in a mesh: gx: 16 (over z, core), gy: 16 (over y, x).
Axes of the slice: x: 4, y: 4, z: 8, core: 2. Of those that a mesh axis runs over, the one named last changes fastest.
Arguments:
- right_side: float32 [256, 256, 512], P('gx', 'gy'), may hold values from -8 to 8
- coefficient: float32 [256, 256, 512], P('gx', 'gy'), may hold values from 0.5 to 4
Outputs:
- solution: float32 [256, 256, 512], P('gx', 'gy')
All inputs are finite; a program needn't handle non-finite values.
Results may differ from a plain program's by a relative error of at most 0.00002.
Values sent between devices are 32-bit elements; how exact they have to be, the bound alone decides.
A program may use at most 128 MiB of HBM per device.

v0:
```python
from functools import partial

import jax
import jax.numpy as jnp
from jax import lax
from jax.sharding import PartitionSpec as P

DEGREE = 2
COARSE_ITERS = 6


cheb_centre = 1.15
cheb_radius = 0.85


def with_halo(value, sides, width):
    for axis, dim in sides:
        devices, length = (lax.axis_size(axis), value.shape[dim])
        up = [(i, (i + 1) % devices) for i in range(devices - 1)]
        down = [(j, i) for i, j in up]
        last = lax.slice_in_dim(value, length - width, length, axis=dim)
        leading = lax.slice_in_dim(value, 0, width, axis=dim)
        before = lax.ppermute(last, axis, up)
        after = lax.ppermute(leading, axis, down)
        value = jnp.concatenate([before, value, after], axis=dim)
    return value


def shifted(value, axis, by):
    devices = lax.axis_size(axis)
    pairs = [(i, i + by) for i in range(devices) if 0 <= i + by < devices]
    return lax.ppermute(value, axis, pairs)


def swapped(value, axis, apart):
    return lax.ppermute(value, axis, [(i, i ^ 1 << apart) for i in range(lax.axis_size(axis))])


def pad_vertical(values):
    return jnp.pad(values, ((0, 0), (0, 0), (1, 1)))


def fine_halo(values):
    return with_halo(values, (("gx", 0), ("gy", 1)), 1)


def group_halo(values, group_size):
    count_y = lax.axis_size("gy")
    place_y = lax.axis_index("gy")
    face_rims = (values[-1:], values[:1], values[:, -1:], values[:, :1])
    offsets = (group_size * count_y, -group_size * count_y, group_size, -group_size)
    keep_masks = (place_y >= 0, place_y >= 0, place_y >= group_size, place_y < count_y - group_size)
    arrived = []
    for face_rim, shift_by, keep_rim in zip(face_rims, offsets, keep_masks):
        moved_rim = shifted(face_rim, ("gx", "gy"), shift_by)
        arrived.append(jnp.where(keep_rim, moved_rim, jnp.zeros_like(moved_rim)))
    along_x = jnp.concatenate((arrived[0], values, arrived[1]), 0)
    lower_y = jnp.pad(arrived[2], ((1, 1), (0, 0), (0, 0)))
    upper_y = jnp.pad(arrived[3], ((1, 1), (0, 0), (0, 0)))
    return jnp.concatenate((lower_y, along_x, upper_y), 1)


def face_weights(padded_coeff):
    center = padded_coeff[1:-1, 1:-1]
    vertical = pad_vertical(center)
    return (
        0.5 * (center + padded_coeff[:-2, 1:-1]),
        0.5 * (center + padded_coeff[2:, 1:-1]),
        0.5 * (center + padded_coeff[1:-1, :-2]),
        0.5 * (center + padded_coeff[1:-1, 2:]),
        0.5 * (center + vertical[:, :, :-2]),
        0.5 * (center + vertical[:, :, 2:]),
    )


def total_weight(weights):
    return weights[0] + weights[1] + weights[2] + weights[3] + weights[4] + weights[5]


def apply_operator(values, padded_coeff, halo_fn):
    padded = halo_fn(values)
    vertical = pad_vertical(values)
    weights = face_weights(padded_coeff)
    beside = (
        weights[0] * padded[:-2, 1:-1]
        + weights[1] * padded[2:, 1:-1]
        + weights[2] * padded[1:-1, :-2]
        + weights[3] * padded[1:-1, 2:]
        + weights[4] * vertical[:, :, :-2]
        + weights[5] * vertical[:, :, 2:]
    )
    return total_weight(weights) * values - beside


def chebyshev(source, initial, steps_count, padded_coeff, inverse_diag, halo_fn):
    rho_previous = cheb_radius / cheb_centre
    if initial is None:
        previous = jnp.zeros_like(source)
        current = inverse_diag * source / cheb_centre
    else:
        previous = initial
        current = (
            initial
            + inverse_diag * (source - apply_operator(initial, padded_coeff, halo_fn)) / cheb_centre
        )
    for turn_index in range(steps_count - 1):
        rho_current = 1.0 / (2.0 * cheb_centre / cheb_radius - rho_previous)
        update = (
            current
            + rho_current * rho_previous * (current - previous)
            + 2.0
            * rho_current
            / cheb_radius
            * inverse_diag
            * (source - apply_operator(current, padded_coeff, halo_fn))
        )
        previous, current, rho_previous = (current, update, rho_current)
    return current


def restrict_sum(values):
    extent = values.shape
    return values.reshape(extent[0] // 2, 2, extent[1] // 2, 2, extent[2] // 2, 2).sum(
        axis=(1, 3, 5)
    )


def prolong(values):
    return jnp.repeat(jnp.repeat(jnp.repeat(values, 2, 0), 2, 1), 2, 2)


def vcycle_step(source, padded, inverse, halo_fn, lower_solve):
    smoothed = chebyshev(source, None, DEGREE, padded, inverse, halo_fn)
    residual = source - apply_operator(smoothed, padded, halo_fn)
    smoothed = smoothed + prolong(lower_solve(0.5 * restrict_sum(residual)))
    return chebyshev(source, smoothed, DEGREE, padded, inverse, halo_fn)


def coarsest_solve(source, level_coeff, halo_fn):
    padded = halo_fn(level_coeff)
    inverse = 1.0 / total_weight(face_weights(padded))
    return chebyshev(source, None, COARSE_ITERS, padded, inverse, halo_fn)


def coarse_cycle(source, level_coeff, halo_fn, coarsest_fn):
    padded = halo_fn(level_coeff)
    inverse = 1.0 / total_weight(face_weights(padded))
    coarse_coeff = 0.125 * restrict_sum(level_coeff)
    return vcycle_step(
        source,
        padded,
        inverse,
        halo_fn,
        lambda coarse_source: coarsest_fn(coarse_source, coarse_coeff),
    )


def join_halves(stacked, linear_bit, concat_dim, place_bits):
    partner = swapped(stacked, ("gx", "gy"), linear_bit)
    lower_half = place_bits & 1 == 0
    first_half = jnp.where(lower_half, stacked, partner)
    second = jnp.where(lower_half, partner, stacked)
    return jnp.concatenate((first_half, second), concat_dim)


def agglomerate(stacked, bit_index):
    span_y = lax.axis_size("gy").bit_length() - 1
    along_x = join_halves(stacked, bit_index + span_y, 1, lax.axis_index("gx") >> bit_index)
    return join_halves(along_x, bit_index, 2, lax.axis_index("gy") >> bit_index)


def own_part(values, bit_index):
    size_x = values.shape[0] // 2
    size_y = values.shape[1] // 2
    start_x = (lax.axis_index("gx") >> bit_index & 1) * size_x
    start_y = (lax.axis_index("gy") >> bit_index & 1) * size_y
    return lax.dynamic_slice(values, (start_x, start_y, 0), (size_x, size_y, values.shape[2]))


def group_lowest(source, level_coeff):
    return coarsest_solve(source, level_coeff, partial(group_halo, group_size=4))


def group_fourth(source, level_coeff):
    stacked = agglomerate(jnp.stack((source, level_coeff)), 1)
    whole_block = coarse_cycle(
        stacked[0], stacked[1], partial(group_halo, group_size=4), group_lowest
    )
    return own_part(whole_block, 1)


def body(right_side, coefficient):
    coeff_levels = [coefficient]
    for level_index in range(2):
        coeff_levels.append(0.125 * restrict_sum(coeff_levels[-1]))
    padded_levels = [fine_halo(values) for values in coeff_levels]
    inverse_levels = [1.0 / total_weight(face_weights(padded)) for padded in padded_levels]
    third_coeff = 0.125 * restrict_sum(coeff_levels[2])

    def coarse_part(coarse_source):
        stacked = agglomerate(jnp.stack((coarse_source, third_coeff)), 0)
        correction = coarse_cycle(
            stacked[0], stacked[1], partial(group_halo, group_size=2), group_fourth
        )
        return own_part(correction, 0)

    def fine_cycle(level_index, source):
        if level_index < 2:
            lower_solve = partial(fine_cycle, level_index + 1)
        else:
            lower_solve = coarse_part
        return vcycle_step(
            source, padded_levels[level_index], inverse_levels[level_index], fine_halo, lower_solve
        )

    return fine_cycle(0, right_side)


def solution(mesh):
    placed = (P("gx", "gy", None), P("gx", "gy", None))
    return jax.shard_map(
        body, mesh=mesh, in_specs=placed, out_specs=P("gx", "gy", None), check_vma=False
    )
```

profile of v0, /device:TPU:119, one launch (start us, length us, event | category | flops | bytes accessed | tf_op | source)
XLA Modules:
  0.0 784.3 jit_solution(10429307171731391760)
XLA Ops:
  31.3 34.8 %reshape.111 = f32[8,2,8,2,256,2]{5,4,3,2,1,0:T(8,128)} reshape(f32[16,16,512]{2,1,0:T(8,128)S(1)} %copy-done) | data formatting | bytes 1048576 | tf_op jit(solution)/shard_map/reshape | solution.py:123
  66.2 12.3 %reduce_sum.90 = f32[8,8,256]{2,1,0:T(8,128)S(1)} reduce(f32[8,2,8,2,256,2]{5,4,3,2,1,0:T(8,128)} %reshape.111, f32[]{:T(128)} %constant.26.clone.1), dimensions={1,3,5}, to_apply=%region_0.0 | reduce | flops 114688 | bytes 589828 | tf_op jit(solution)/shard_map/reduce_sum | solution.py:123
  92.2 6.0 collective-permute-start.12
  119.9 35.6 %reshape.112 = f32[8,2,8,2,256,2]{5,4,3,2,1,0:T(8,128)} reshape(f32[16,16,512]{2,1,0:T(8,128)} %fusion.16) | data formatting | bytes 1048576 | tf_op jit(solution)/shard_map/reshape | solution.py:123
  155.4 12.2 %reduce_sum.91 = f32[8,8,256]{2,1,0:T(8,128)S(1)} reduce(f32[8,2,8,2,256,2]{5,4,3,2,1,0:T(8,128)} %reshape.112, f32[]{:T(128)} %constant.26.clone.1), dimensions={1,3,5}, to_apply=%region_1.0 | reduce | flops 114688 | bytes 589828 | tf_op jit(solution)/shard_map/reduce_sum | solution.py:123
  177.1 5.5 mul.1138
  186.5 5.8 collective-permute-start.18
  200.2 6.3 collective-permute-start.24
  229.2 6.3 reshape.113
  250.4 5.8 collective-permute-start.30
  320.6 5.8 collective-permute-start.44
  335.7 5.8 collective-permute-start.48
  368.9 7.1 collective-permute-start.54
  396.5 6.4 collective-permute-done.63
  402.9 8.9 %collective-permute-start.62 = (f32[2,1,16]{2,1,0:T(1,128)S(1)}, f32[2,1,16]{2,1,0:T(1,128)S(1)}, u32[]{:S(2)}, u32[]{:S(2)}) collective-permute-start(f32[2,1,16]{2,1,0:T(1,128)S(1)} %get-tuple-element.173), channel_id=1, source_target_pairs={{0,4},{1,5},{2,6},{3,7},{4,8},{5,9},{6,10},{7,11},{8,12},{9,13},{1... | collective-permute-start | bytes 392 | tf_op jit(solution)/shard_map/ppermute | solution.py:32
  428.6 5.9 collective-permute-done.59
  435.4 7.3 collective-permute-start.66
  444.6 5.5 collective-permute-start.64
  460.0 5.8 collective-permute-start.70
  467.8 5.5 collective-permute-start.68
  478.4 5.8 collective-permute-start.74
  486.2 5.5 collective-permute-start.72
  496.7 5.9 collective-permute-start.78
  504.5 5.5 collective-permute-start.76
  515.1 5.9 collective-permute-start.82
  522.9 5.5 collective-permute-start.80
  533.4 5.9 collective-permute-start.86
  541.2 5.5 collective-permute-start.84
  557.5 5.9 collective-permute-start.90
  565.3 5.5 collective-permute-start.88
  578.7 5.5 collective-permute-start.92
  584.2 5.9 collective-permute-start.94
  (557 shorter events, 519.1 us)
Async XLA Ops:
  26.0 52.4 %collective-permute-start.4 = (f32[1,16,512]{2,1,0:T(8,128)S(1)}, f32[1,16,512]{2,1,0:T(8,128)S(1)}, u32[]{:S(2)}, u32[]{:S(2)}) collective-permute-start(f32[1,16,512]{2,1,0:T(8,128)S(1)} %get-tuple-element.56), channel_id=1, source_target_pairs={{0,16},{16,32},{32,48},{48,64},{64,80},{80,96},{96,112},{112,128},... | collective-permute-start | bytes 98312 | tf_op jit(solution)/shard_map/ppermute | solution.py:23
  29.4 49.1 %collective-permute-start.5 = (f32[1,16,512]{2,1,0:T(8,128)S(1)}, f32[1,16,512]{2,1,0:T(8,128)S(1)}, u32[]{:S(2)}, u32[]{:S(2)}) collective-permute-start(f32[1,16,512]{2,1,0:T(8,128)S(1)} %get-tuple-element.57), channel_id=1, source_target_pairs={{16,0},{32,16},{48,32},{64,48},{80,64},{96,80},{112,96},{128,112},... | collective-permute-start | bytes 98312 | tf_op jit(solution)/shard_map/ppermute | solution.py:24
  92.2 14.7 %collective-permute-start.12 = (f32[1,16,512]{2,1,0:T(8,128)S(1)}, f32[1,16,512]{2,1,0:T(8,128)S(1)}, u32[]{:S(2)}, u32[]{:S(2)}) collective-permute-start(f32[1,16,512]{2,1,0:T(8,128)S(1)} %get-tuple-element.54), channel_id=1, source_target_pairs={{0,16},{16,32},{32,48},{48,64},{64,80},{80,96},{96,112},{112,128},... | collective-permute-start | bytes 98312 | tf_op jit(solution)/shard_map/ppermute | solution.py:23
  112.4 55.3 %collective-permute-start.10 = (f32[10,1,256]{2,1,0:T(1,128)S(1)}, f32[10,1,256]{2,1,0:T(1,128)S(1)}, u32[]{:S(2)}, u32[]{:S(2)}) collective-permute-start(f32[10,1,256]{2,1,0:T(1,128)S(1)} %get-tuple-element.69), channel_id=1, source_target_pairs={{0,1},{1,2},{2,3},{3,4},{4,5},{5,6},{6,7},{7,8},{8,9},{9,10},{10,1... | collective-permute-start | bytes 30728 | tf_op jit(solution)/shard_map/ppermute | solution.py:23
  116.4 51.9 %collective-permute-start.11 = (f32[10,1,256]{2,1,0:T(1,128)S(1)}, f32[10,1,256]{2,1,0:T(1,128)}, u32[]{:S(2)}, u32[]{:S(2)}) collective-permute-start(f32[10,1,256]{2,1,0:T(1,128)S(1)} %get-tuple-element.68), channel_id=1, source_target_pairs={{1,0},{2,1},{3,2},{4,3},{5,4},{6,5},{7,6},{8,7},{9,8},{10,9},{11,1... | collective-permute-start | bytes 30728 | tf_op jit(solution)/shard_map/ppermute | solution.py:24
  169.7 16.0 %collective-permute-start.16 = (f32[1,8,256]{2,1,0:T(8,128)}, f32[1,8,256]{2,1,0:T(8,128)S(1)}, u32[]{:S(2)}, u32[]{:S(2)}) collective-permute-start(f32[1,8,256]{2,1,0:T(8,128)} %get-tuple-element.76), channel_id=1, source_target_pairs={{0,16},{16,32},{32,48},{48,64},{64,80},{80,96},{96,112},{112,128},... | collective-permute-start | bytes 24584 | tf_op jit(solution)/shard_map/ppermute | solution.py:23
  200.2 15.0 %collective-permute-start.24 = (f32[1,8,256]{2,1,0:T(8,128)S(1)}, f32[1,8,256]{2,1,0:T(8,128)S(1)}, u32[]{:S(2)}, u32[]{:S(2)}) collective-permute-start(f32[1,8,256]{2,1,0:T(8,128)S(1)} %get-tuple-element.74), channel_id=1, source_target_pairs={{0,16},{16,32},{32,48},{48,64},{64,80},{80,96},{96,112},{112,128},... | collective-permute-start | bytes 24584 | tf_op jit(solution)/shard_map/ppermute | solution.py:23
  215.2 12.5 %collective-permute-start.26 = (f32[10,1,256]{2,1,0:T(1,128)S(1)}, f32[10,1,256]{2,1,0:T(1,128)S(1)}, u32[]{:S(2)}, u32[]{:S(2)}) collective-permute-start(f32[10,1,256]{2,1,0:T(1,128)S(1)} %get-tuple-element.64), channel_id=1, source_target_pairs={{0,1},{1,2},{2,3},{3,4},{4,5},{5,6},{6,7},{7,8},{8,9},{9,10},{10,1... | collective-permute-start | bytes 30728 | tf_op jit(solution)/shard_map/ppermute | solution.py:23
  221.7 16.3 %collective-permute-start.22 = (f32[6,1,128]{2,1,0:T(1,128)}, f32[6,1,128]{2,1,0:T(1,128)}, u32[]{:S(2)}, u32[]{:S(2)}) collective-permute-start(f32[6,1,128]{2,1,0:T(1,128)} %get-tuple-element.97), channel_id=1, source_target_pairs={{0,1},{1,2},{2,3},{3,4},{4,5},{5,6},{6,7},{7,8},{8,9},{9,10},{10,1... | collective-permute-start | bytes 9224 | tf_op jit(solution)/shard_map/ppermute | solution.py:23
  225.8 12.3 %collective-permute-start.23 = (f32[6,1,128]{2,1,0:T(1,128)}, f32[6,1,128]{2,1,0:T(1,128)}, u32[]{:S(2)}, u32[]{:S(2)}) collective-permute-start(f32[6,1,128]{2,1,0:T(1,128)} %get-tuple-element.96), channel_id=1, source_target_pairs={{1,0},{2,1},{3,2},{4,3},{5,4},{6,5},{7,6},{8,7},{9,8},{10,9},{11,1... | collective-permute-start | bytes 9224 | tf_op jit(solution)/shard_map/ppermute | solution.py:24
  299.2 17.3 %collective-permute-start.41 = (f32[4,1,64]{2,1,0:T(1,128)}, f32[4,1,64]{2,1,0:T(1,128)}, u32[]{:S(2)}, u32[]{:S(2)}) collective-permute-start(f32[4,1,64]{2,1,0:T(1,128)} %get-tuple-element.142), channel_id=1, source_target_pairs={{2,0},{3,1},{4,2},{5,3},{6,4},{7,5},{8,6},{9,7},{10,8},{11,9},{12,... | collective-permute-start | bytes 3080 | tf_op jit(solution)/shard_map/ppermute | solution.py:32
  301.9 15.3 %collective-permute-start.40 = (f32[4,1,64]{2,1,0:T(1,128)}, f32[4,1,64]{2,1,0:T(1,128)}, u32[]{:S(2)}, u32[]{:S(2)}) collective-permute-start(f32[4,1,64]{2,1,0:T(1,128)} %get-tuple-element.143), channel_id=1, source_target_pairs={{0,2},{1,3},{2,4},{3,5},{4,6},{5,7},{6,8},{7,9},{8,10},{9,11},{10,... | collective-permute-start | bytes 3080 | tf_op jit(solution)/shard_map/ppermute | solution.py:32
  318.7 14.2 %collective-permute-start.45 = (f32[4,1,64]{2,1,0:T(1,128)S(1)}, f32[4,1,64]{2,1,0:T(1,128)S(1)}, u32[]{:S(2)}, u32[]{:S(2)}) collective-permute-start(f32[4,1,64]{2,1,0:T(1,128)S(1)} %get-tuple-element.139), channel_id=1, source_target_pairs={{2,0},{3,1},{4,2},{5,3},{6,4},{7,5},{8,6},{9,7},{10,8},{11,9},{12,... | collective-permute-start | bytes 3080 | tf_op jit(solution)/shard_map/ppermute | solution.py:32
  320.6 12.3 %collective-permute-start.44 = (f32[4,1,64]{2,1,0:T(1,128)S(1)}, f32[4,1,64]{2,1,0:T(1,128)S(1)}, u32[]{:S(2)}, u32[]{:S(2)}) collective-permute-start(f32[4,1,64]{2,1,0:T(1,128)S(1)} %get-tuple-element.138), channel_id=1, source_target_pairs={{0,2},{1,3},{2,4},{3,5},{4,6},{5,7},{6,8},{7,9},{8,10},{9,11},{10,... | collective-permute-start | bytes 3080 | tf_op jit(solution)/shard_map/ppermute | solution.py:32
  333.7 14.5 %collective-permute-start.49 = (f32[4,1,64]{2,1,0:T(1,128)S(1)}, f32[4,1,64]{2,1,0:T(1,128)S(1)}, u32[]{:S(2)}, u32[]{:S(2)}) collective-permute-start(f32[4,1,64]{2,1,0:T(1,128)S(1)} %get-tuple-element.135), channel_id=1, source_target_pairs={{2,0},{3,1},{4,2},{5,3},{6,4},{7,5},{8,6},{9,7},{10,8},{11,9},{12,... | collective-permute-start | bytes 3080 | tf_op jit(solution)/shard_map/ppermute | solution.py:32
  335.7 12.6 %collective-permute-start.48 = (f32[4,1,64]{2,1,0:T(1,128)S(1)}, f32[4,1,64]{2,1,0:T(1,128)S(1)}, u32[]{:S(2)}, u32[]{:S(2)}) collective-permute-start(f32[4,1,64]{2,1,0:T(1,128)S(1)} %get-tuple-element.134), channel_id=1, source_target_pairs={{0,2},{1,3},{2,4},{3,5},{4,6},{5,7},{6,8},{7,9},{8,10},{9,11},{10,... | collective-permute-start | bytes 3080 | tf_op jit(solution)/shard_map/ppermute | solution.py:32
  368.9 44.3 %collective-permute-start.54 = (f32[4,1,32]{2,1,0:T(1,128)S(1)}, f32[4,1,32]{2,1,0:T(1,128)S(1)}, u32[]{:S(2)}, u32[]{:S(2)}) collective-permute-start(f32[4,1,32]{2,1,0:T(1,128)S(1)} %get-tuple-element.131), channel_id=1, source_target_pairs={{0,4},{1,5},{2,6},{3,7},{4,8},{5,9},{6,10},{7,11},{8,12},{9,13},{1... | collective-permute-start | bytes 1544 | tf_op jit(solution)/shard_map/ppermute | solution.py:32
  375.9 37.2 %collective-permute-start.52 = (f32[1,4,32]{2,1,0:T(4,128)}, f32[1,4,32]{2,1,0:T(4,128)S(1)}, u32[]{:S(2)}, u32[]{:S(2)}) collective-permute-start(f32[1,4,32]{2,1,0:T(4,128)} %get-tuple-element.80), channel_id=1, source_target_pairs={{0,64},{1,65},{2,66},{3,67},{4,68},{5,69},{6,70},{7,71},{8,72},{9,... | collective-permute-start | bytes 1544 | tf_op jit(solution)/shard_map/ppermute | solution.py:32
  380.4 32.7 %collective-permute-start.55 = (f32[4,1,32]{2,1,0:T(1,128)S(1)}, f32[4,1,32]{2,1,0:T(1,128)S(1)}, u32[]{:S(2)}, u32[]{:S(2)}) collective-permute-start(f32[4,1,32]{2,1,0:T(1,128)S(1)} %get-tuple-element.130), channel_id=1, source_target_pairs={{4,0},{5,1},{6,2},{7,3},{8,4},{9,5},{10,6},{11,7},{12,8},{13,9},{1... | collective-permute-start | bytes 1544 | tf_op jit(solution)/shard_map/ppermute | solution.py:32
  384.3 28.9 %collective-permute-start.53 = (f32[1,4,32]{2,1,0:T(4,128)}, f32[1,4,32]{2,1,0:T(4,128)S(1)}, u32[]{:S(2)}, u32[]{:S(2)}) collective-permute-start(f32[1,4,32]{2,1,0:T(4,128)} %get-tuple-element.81), channel_id=1, source_target_pairs={{64,0},{65,1},{66,2},{67,3},{68,4},{69,5},{70,6},{71,7},{72,8},{73... | collective-permute-start | bytes 1544 | tf_op jit(solution)/shard_map/ppermute | solution.py:32
  414.4 14.2 %collective-permute-start.58 = (f32[4,1,32]{2,1,0:T(1,128)S(1)}, f32[4,1,32]{2,1,0:T(1,128)S(1)}, u32[]{:S(2)}, u32[]{:S(2)}) collective-permute-start(f32[4,1,32]{2,1,0:T(1,128)S(1)} %get-tuple-element.126), channel_id=1, source_target_pairs={{0,4},{1,5},{2,6},{3,7},{4,8},{5,9},{6,10},{7,11},{8,12},{9,13},{1... | collective-permute-start | bytes 1544 | tf_op jit(solution)/shard_map/ppermute | solution.py:32
  435.4 16.6 %collective-permute-start.66 = (f32[4,1,32]{2,1,0:T(1,128)S(1)}, f32[4,1,32]{2,1,0:T(1,128)S(1)}, u32[]{:S(2)}, u32[]{:S(2)}) collective-permute-start(f32[4,1,32]{2,1,0:T(1,128)S(1)} %get-tuple-element.122), channel_id=1, source_target_pairs={{0,4},{1,5},{2,6},{3,7},{4,8},{5,9},{6,10},{7,11},{8,12},{9,13},{1... | collective-permute-start | bytes 1544 | tf_op jit(solution)/shard_map/ppermute | solution.py:32
  460.0 15.2 %collective-permute-start.70 = (f32[2,1,16]{2,1,0:T(1,128)S(1)}, f32[2,1,16]{2,1,0:T(1,128)S(1)}, u32[]{:S(2)}, u32[]{:S(2)}) collective-permute-start(f32[2,1,16]{2,1,0:T(1,128)S(1)} %get-tuple-element.168), channel_id=1, source_target_pairs={{0,4},{1,5},{2,6},{3,7},{4,8},{5,9},{6,10},{7,11},{8,12},{9,13},{1... | collective-permute-start | bytes 392 | tf_op jit(solution)/shard_map/ppermute | solution.py:32
  478.4 15.2 %collective-permute-start.74 = (f32[2,1,16]{2,1,0:T(1,128)S(1)}, f32[2,1,16]{2,1,0:T(1,128)S(1)}, u32[]{:S(2)}, u32[]{:S(2)}) collective-permute-start(f32[2,1,16]{2,1,0:T(1,128)S(1)} %get-tuple-element.164), channel_id=1, source_target_pairs={{0,4},{1,5},{2,6},{3,7},{4,8},{5,9},{6,10},{7,11},{8,12},{9,13},{1... | collective-permute-start | bytes 392 | tf_op jit(solution)/shard_map/ppermute | solution.py:32
  496.7 15.2 %collective-permute-start.78 = (f32[2,1,16]{2,1,0:T(1,128)S(1)}, f32[2,1,16]{2,1,0:T(1,128)S(1)}, u32[]{:S(2)}, u32[]{:S(2)}) collective-permute-start(f32[2,1,16]{2,1,0:T(1,128)S(1)} %get-tuple-element.160), channel_id=1, source_target_pairs={{0,4},{1,5},{2,6},{3,7},{4,8},{5,9},{6,10},{7,11},{8,12},{9,13},{1... | collective-permute-start | bytes 392 | tf_op jit(solution)/shard_map/ppermute | solution.py:32
  515.1 15.2 %collective-permute-start.82 = (f32[2,1,16]{2,1,0:T(1,128)S(1)}, f32[2,1,16]{2,1,0:T(1,128)S(1)}, u32[]{:S(2)}, u32[]{:S(2)}) collective-permute-start(f32[2,1,16]{2,1,0:T(1,128)S(1)} %get-tuple-element.156), channel_id=1, source_target_pairs={{0,4},{1,5},{2,6},{3,7},{4,8},{5,9},{6,10},{7,11},{8,12},{9,13},{1... | collective-permute-start | bytes 392 | tf_op jit(solution)/shard_map/ppermute | solution.py:32
  533.4 15.2 %collective-permute-start.86 = (f32[2,1,16]{2,1,0:T(1,128)S(1)}, f32[2,1,16]{2,1,0:T(1,128)S(1)}, u32[]{:S(2)}, u32[]{:S(2)}) collective-permute-start(f32[2,1,16]{2,1,0:T(1,128)S(1)} %get-tuple-element.152), channel_id=1, source_target_pairs={{0,4},{1,5},{2,6},{3,7},{4,8},{5,9},{6,10},{7,11},{8,12},{9,13},{1... | collective-permute-start | bytes 392 | tf_op jit(solution)/shard_map/ppermute | solution.py:32
  557.5 15.2 %collective-permute-start.90 = (f32[4,1,32]{2,1,0:T(1,128)S(1)}, f32[4,1,32]{2,1,0:T(1,128)S(1)}, u32[]{:S(2)}, u32[]{:S(2)}) collective-permute-start(f32[4,1,32]{2,1,0:T(1,128)S(1)} %get-tuple-element.118), channel_id=1, source_target_pairs={{0,4},{1,5},{2,6},{3,7},{4,8},{5,9},{6,10},{7,11},{8,12},{9,13},{1... | collective-permute-start | bytes 1544 | tf_op jit(solution)/shard_map/ppermute | solution.py:32
  576.8 15.2 %collective-permute-start.93 = (f32[1,4,32]{2,1,0:T(4,128)S(1)}, f32[1,4,32]{2,1,0:T(4,128)S(1)}, u32[]{:S(2)}, u32[]{:S(2)}) collective-permute-start(f32[1,4,32]{2,1,0:T(4,128)S(1)} %get-tuple-element.117), channel_id=1, source_target_pairs={{64,0},{65,1},{66,2},{67,3},{68,4},{69,5},{70,6},{71,7},{72,8},{73... | collective-permute-start | bytes 1544 | tf_op jit(solution)/shard_map/ppermute | solution.py:32
  578.7 13.3 %collective-permute-start.92 = (f32[1,4,32]{2,1,0:T(4,128)S(1)}, f32[1,4,32]{2,1,0:T(4,128)S(1)}, u32[]{:S(2)}, u32[]{:S(2)}) collective-permute-start(f32[1,4,32]{2,1,0:T(4,128)S(1)} %get-tuple-element.116), channel_id=1, source_target_pairs={{0,64},{1,65},{2,66},{3,67},{4,68},{5,69},{6,70},{7,71},{8,72},{9,... | collective-permute-start | bytes 1544 | tf_op jit(solution)/shard_map/ppermute | solution.py:32
  601.8 13.7 %collective-permute-start.98 = (f32[4,1,64]{2,1,0:T(1,128)S(1)}, f32[4,1,64]{2,1,0:T(1,128)S(1)}, u32[]{:S(2)}, u32[]{:S(2)}) collective-permute-start(f32[4,1,64]{2,1,0:T(1,128)S(1)} %get-tuple-element.108), channel_id=1, source_target_pairs={{0,2},{1,3},{2,4},{3,5},{4,6},{5,7},{6,8},{7,9},{8,10},{9,11},{10,... | collective-permute-start | bytes 3080 | tf_op jit(solution)/shard_map/ppermute | solution.py:32
  622.0 13.3 %collective-permute-start.102 = (f32[4,1,64]{2,1,0:T(1,128)S(1)}, f32[4,1,64]{2,1,0:T(1,128)S(1)}, u32[]{:S(2)}, u32[]{:S(2)}) collective-permute-start(f32[4,1,64]{2,1,0:T(1,128)S(1)} %get-tuple-element.104), channel_id=1, source_target_pairs={{0,2},{1,3},{2,4},{3,5},{4,6},{5,7},{6,8},{7,9},{8,10},{9,11},{10,... | collective-permute-start | bytes 3080 | tf_op jit(solution)/shard_map/ppermute | solution.py:32
  (145 other events, 1876.5 us)
where the time goes:
time: 791 us; the launch traced here: 784 us
  starting transfers between devices  414 us (52%)
  local copies, waits for them, and re-layouts  133 us (17%)
  waiting for transfers between devices  131 us (17%)
  other arithmetic  102 us (13%)
    ppermute x64, starting transfers between devices, shifted(): return lax.ppermute(value, axis, pairs)  236 us
    ppermute x30, starting transfers between devices, with_halo(): before = lax.ppermute(last, axis, up)  107 us
    reshape x6, local copies, waits for them, and re-layouts, restrict_sum(): values.reshape(extent[0] // 2, 2, extent[1] // 2, 2, extent[2] // 2, 2)  81.8 us
    ppermute x30, waiting for transfers between devices, with_halo(): after = lax.ppermute(leading, axis, down)  74.8 us
    ppermute x30, starting transfers between devices, with_halo(): after = lax.ppermute(leading, axis, down)  71.1 us
    ppermute x64, waiting for transfers between devices, shifted(): return lax.ppermute(value, axis, pairs)  46.5 us
    reduce_sum x10, other arithmetic, restrict_sum(): values.reshape(extent[0] // 2, 2, extent[1] // 2, 2, extent[2] // 2, 2)  40.1 us
    reshape x11, local copies, waits for them, and re-layouts, prolong(): return jnp.repeat(jnp.repeat(jnp.repeat(values, 2, 0), 2, 1), 2, 2)  19.8 us
  transfers between devices with their start and end apart: 128, of which 41 were waited for; matrix products, arithmetic and copies ran while one was open for 17% of the time, Pallas kernels for 0%

commit v1 on v0

v1 whole, which is shorter than its diff:
```python
import functools

import jax
import jax.numpy as jnp
from jax import lax
from jax.experimental import pallas as pl
from jax.experimental.pallas import tpu as pltpu
from jax.sharding import PartitionSpec as P

MESH = pl.DeviceIdType.MESH
F32 = jnp.float32
BF16 = jnp.bfloat16

CENTRE = 1.15
RADIUS = 0.85
COARSE_ITERS = 6
SIGMA = CENTRE / RADIUS
RHO0 = 1.0 / SIGMA
RHO1 = 1.0 / (2.0 * SIGMA - RHO0)
KEEP = 1.0 + RHO1 * RHO0 - 2.0 * RHO1 / RADIUS
OLD = RHO1 * RHO0
STEP = 2.0 * RHO1 / RADIUS
FIRST = 1.0 / CENTRE

NEIGHBOURS = [(dx, dy) for dx in (-1, 0, 1) for dy in (-1, 0, 1) if (dx, dy) != (0, 0)]
ROW0 = 8
LANES = 128


class Fine:
    def __init__(self, parts, n, off, rows, halo_inv):
        self.parts, self.n, self.off, self.rows, self.halo_inv = parts, n, off, rows, halo_inv
        self.planes = n + 2 * off
        self.shape = (parts, self.planes, rows, LANES)

    def tiles(self, halo):
        low, count = ROW0 - halo, self.n + 2 * halo
        if halo == 0:
            return [low + 8 * t for t in range(-(-count // 8))]
        if count % 8 == 0:
            return [low + 8 * t for t in range(count // 8)]
        tiles = -(-count // 8)
        low -= (tiles * 8 - count) // 2
        return [low + 8 * t for t in range(tiles)]


class Coarse:
    def __init__(self, planes, n, step, split):
        self.planes, self.n, self.step, self.split = planes, n, step, split
        self.shape = (planes + 2, n + 16, LANES)
        self.tiles = [ROW0 + 8 * t for t in range(n // 8)]


L0 = Fine(4, 16, 4, 32, 2)
L1 = Fine(2, 8, 6, 24, 4)
L2 = Fine(1, 4, 5, 24, 3)


def roll(value, by):
    return pltpu.roll(value, by % LANES, 1)


def lane_iota():
    return lax.broadcasted_iota(jnp.int32, (8, LANES), 1)


def loop(count, step, fn):
    assert count % step == 0

    def turn(i, carry):
        for k in range(step):
            fn(i * step + k)
        return carry

    lax.fori_loop(0, count // step, turn, 0)


def split3(value):
    high = value.astype(BF16)
    rest = value - high.astype(F32)
    mid = rest.astype(BF16)
    low = (rest - mid.astype(F32)).astype(BF16)
    return high, mid, low


def exact_dot(value, matrix):
    total = None
    for part in split3(value):
        term = jnp.dot(part, matrix, preferred_element_type=F32)
        total = term if total is None else total + term
    return total


def fine_setup(lv, k_ref, w, gx, gy, size_x, size_y):
    wx, wy, wz, inv, diag = w
    h = lv.halo_inv
    lane = lane_iota()
    row = lax.broadcasted_iota(jnp.int32, (8, LANES), 0)
    parts = lv.parts

    def plane(i):
        x = lv.off - h + i
        gx_cell = gx * lv.n + (i - h)
        in_x = jnp.logical_and(gx_cell >= 0, gx_cell < size_x)
        for r in lv.tiles(h):
            cells = [k_ref[p, x, pl.ds(r, 8), :] for p in range(parts)]
            gy_cell = gy * lv.n + (r - ROW0) + row
            inside = jnp.logical_and(jnp.logical_and(gy_cell >= 0, gy_cell < size_y), in_x)
            first = jnp.where(lane == 0, 0.0, roll(cells[parts - 1], 1))
            last = jnp.where(lane == LANES - 1, 0.0, roll(cells[0], -1))
            for p in range(parts):
                k = cells[p]
                kxm = k_ref[p, x - 1, pl.ds(r, 8), :]
                kxp = k_ref[p, x + 1, pl.ds(r, 8), :]
                kym = k_ref[p, x, pl.ds(r - 1, 8), :]
                kyp = k_ref[p, x, pl.ds(r + 1, 8), :]
                kzm = first if p == 0 else cells[p - 1]
                kzp = last if p == parts - 1 else cells[p + 1]
                wx[p, x, pl.ds(r, 8), :] = 0.5 * (k + kxm)
                wy[p, x, pl.ds(r, 8), :] = 0.5 * (k + kym)
                down = 0.5 * (k + kzm)
                if p == 0:
                    down = jnp.where(lane == 0, 0.0, down)
                    wz[parts, x, pl.ds(r, 8), :] = roll(down, -1)
                wz[p, x, pl.ds(r, 8), :] = down
                d = 3.0 * k + 0.5 * (((kxm + kxp) + (kym + kyp)) + (kzm + kzp))
                diag[p, x, pl.ds(r, 8), :] = d
                inv[p, x, pl.ds(r, 8), :] = jnp.where(inside, 1.0 / d, 0.0)

    count = lv.n + 2 * h + 1
    loop(count, 1, plane)


def fine_sum(lv, v_ref, w, x, r):
    wx, wy, wz = w[0], w[1], w[2]
    parts = lv.parts
    cells = [v_ref[p, x, pl.ds(r, 8), :] for p in range(parts)]
    below, above = roll(cells[parts - 1], 1), roll(cells[0], -1)
    sums = []
    for p in range(parts):
        along_x = (
            wx[p, x, pl.ds(r, 8), :] * v_ref[p, x - 1, pl.ds(r, 8), :]
            + wx[p, x + 1, pl.ds(r, 8), :] * v_ref[p, x + 1, pl.ds(r, 8), :]
        )
        along_y = (
            wy[p, x, pl.ds(r, 8), :] * v_ref[p, x, pl.ds(r - 1, 8), :]
            + wy[p, x, pl.ds(r + 1, 8), :] * v_ref[p, x, pl.ds(r + 1, 8), :]
        )
        along_z = wz[p, x, pl.ds(r, 8), :] * (below if p == 0 else cells[p - 1]) + wz[
            p + 1, x, pl.ds(r, 8), :
        ] * (above if p == parts - 1 else cells[p + 1])
        sums.append((along_x + along_y) + along_z)
    return sums, cells


def fine_first(lv, b_ref, w, out_ref, halo):
    inv = w[3]

    def plane(i):
        x = lv.off - halo + i
        for r in lv.tiles(halo):
            for p in range(lv.parts):
                at = (p, x, pl.ds(r, 8), slice(None))
                out_ref[at] = FIRST * (inv[at] * b_ref[at])

    loop(lv.n + 2 * halo, 2, plane)


def fine_step(lv, b_ref, w, v_ref, old_ref, out_ref, halo, keep, old, step):
    inv = w[3]

    def plane(i):
        x = lv.off - halo + i
        for r in lv.tiles(halo):
            sums, cells = fine_sum(lv, v_ref, w, x, r)
            for p in range(lv.parts):
                at = (p, x, pl.ds(r, 8), slice(None))
                value = keep * cells[p] + step * (inv[at] * (b_ref[at] + sums[p]))
                if old_ref is not None:
                    value = value - old * old_ref[at]
                out_ref[at] = value

    loop(lv.n + 2 * halo, 2, plane)


def fine_restrict(lv, b_ref, w, v_ref, tmp_ref):
    diag = w[4]
    parts = lv.parts

    def pair(i):
        for r in lv.tiles(0):
            total = [None] * max(parts // 2, 1)
            for k in range(2):
                x = lv.off + 2 * i + k
                sums, cells = fine_sum(lv, v_ref, w, x, r)
                for p in range(parts):
                    at = (p, x, pl.ds(r, 8), slice(None))
                    res = (b_ref[at] + sums[p]) - diag[at] * cells[p]
                    q = p // 2
                    total[q] = res if total[q] is None else total[q] + res
            for q, value in enumerate(total):
                tmp_ref[q, i, pl.ds(r - ROW0, 8), :] = value

    loop(lv.n // 2, 1, pair)


def fold_x(lv, k_ref, tmp_ref):
    def pair(i):
        for r in lv.tiles(0):
            for q in range(max(lv.parts // 2, 1)):
                total = None
                for p in range(lv.parts):
                    if p // 2 == q:
                        for k in range(2):
                            value = k_ref[p, lv.off + 2 * i + k, pl.ds(r, 8), :]
                            total = value if total is None else total + value
                tmp_ref[q, i, pl.ds(r - ROW0, 8), :] = total

    loop(lv.n // 2, 1, pair)


def fold_y(lv, tmp_ref, out_ref, off, scale):
    half = lv.n // 2
    for q in range(lv.parts // 2):
        for i in range(half):
            even = tmp_ref[q, i, pl.ds(0, half, stride=2), :]
            odd = tmp_ref[q, i, pl.ds(1, half, stride=2), :]
            out_ref[q, off + i, pl.ds(ROW0, half), :] = scale * (even + odd)


def fold_z(tmp_ref, left_ref, matrix, scale):
    for i in range(2):
        for j in range(2):
            row = tmp_ref[0, i, pl.ds(2 * j, 1), :] + tmp_ref[0, i, pl.ds(2 * j + 1, 1), :]
            left_ref[pl.ds(i, 1), pl.ds(LANES * j, LANES)] = scale * row
    return exact_dot(left_ref[...], matrix)


def fine_correct(lv, next_lv, e_ref, s_ref, t_ref, halo):
    next_halo = -(-halo // 2)
    row_lo = ROW0 - next_halo
    rows = next_lv.n + 2 * next_halo
    starts = [row_lo + 8 * t for t in range(-(-rows // 8))]
    if len(starts) == 2:
        starts = [4, 12]

    def plane(i):
        big = next_lv.off - next_halo + i
        for q in range(next_lv.parts):
            for r in starts:
                e = e_ref[q, big, pl.ds(r, 8), :]
                base = 2 * (r - ROW0) + ROW0
                for p in (2 * q, 2 * q + 1):
                    for k in range(2):
                        x = lv.off + 2 * (i - next_halo) + k
                        for c in range(2):
                            at = (p, x, pl.ds(base + c, 8, stride=2), slice(None))
                            t_ref[at] = s_ref[at] + e

    loop(next_lv.n + 2 * next_halo, 1, plane)


def coarse_rolls(lv, ref, first, count, r):
    return [roll(ref[first - 1 + i, pl.ds(r, 8), :], LANES // 2) for i in range(count + 2)]


def coarse_beside(lv, ref, first, count, r):
    out = []
    low = lane_iota() < LANES // 2
    turned = coarse_rolls(lv, ref, first, count, r) if lv.split else None
    for i in range(count):
        y = first + i
        v = ref[y, pl.ds(r, 8), :]
        xm, xp = ref[y, pl.ds(r - 1, 8), :], ref[y, pl.ds(r + 1, 8), :]
        if lv.split:
            ym = jnp.where(low, turned[i], turned[i + 1])
            yp = jnp.where(low, turned[i + 1], turned[i + 2])
        else:
            ym, yp = ref[y - 1, pl.ds(r, 8), :], ref[y + 1, pl.ds(r, 8), :]
        out.append((v, xm, xp, ym, yp, roll(v, lv.step), roll(v, -lv.step)))
    return out


def coarse_setup(lv, k_ref, w):
    lane = lane_iota() % (LANES // 2)
    bottom, top = lane < lv.step, lane >= LANES // 2 - lv.step
    group = 2

    def planes(i):
        first = 1 + group * i
        for r in lv.tiles:
            for j, (k, xm, xp, ym, yp, zm, zp) in enumerate(
                coarse_beside(lv, k_ref, first, group, r)
            ):
                y = first + j
                zm, zp = jnp.where(bottom, 0.0, zm), jnp.where(top, 0.0, zp)
                w[0][0, y, pl.ds(r, 8), :] = 0.5 * (k + xm)
                w[0][1, y, pl.ds(r, 8), :] = 0.5 * (k + xp)
                w[0][2, y, pl.ds(r, 8), :] = 0.5 * (k + ym)
                w[0][3, y, pl.ds(r, 8), :] = 0.5 * (k + yp)
                w[0][4, y, pl.ds(r, 8), :] = jnp.where(bottom, 0.0, 0.5 * (k + zm))
                w[0][5, y, pl.ds(r, 8), :] = jnp.where(top, 0.0, 0.5 * (k + zp))
                d = 3.0 * k + 0.5 * (((xm + xp) + (ym + yp)) + (zm + zp))
                w[0][6, y, pl.ds(r, 8), :] = d
                w[0][7, y, pl.ds(r, 8), :] = 1.0 / d

    loop(lv.planes // group, 1, planes)


def coarse_apply(lv, w, v_ref, fn, group=4):
    def planes(i):
        first = 1 + group * i
        for r in lv.tiles:
            for j, beside in enumerate(coarse_beside(lv, v_ref, first, group, r)):
                y = first + j
                total = None
                for f in range(6):
                    term = w[0][f, y, pl.ds(r, 8), :] * beside[1 + f]
                    total = term if total is None else total + term
                fn(y, r, beside[0], total)

    loop(lv.planes // group, 1, planes)


def coarse_first(lv, b_ref, w, out_ref):
    def plane(i):
        for r in lv.tiles:
            at = (1 + i, pl.ds(r, 8), slice(None))
            out_ref[at] = FIRST * (w[0][7, 1 + i, pl.ds(r, 8), :] * b_ref[at])

    loop(lv.planes, 4, plane)


def coarse_step(lv, b_ref, w, v_ref, old_ref, out_ref, keep, old, step):
    def tile(y, r, v, total):
        at = (y, pl.ds(r, 8), slice(None))
        value = keep * v + step * (w[0][7, y, pl.ds(r, 8), :] * (b_ref[at] + total))
        if old_ref is not None:
            value = value - old * old_ref[at]
        out_ref[at] = value

    coarse_apply(lv, w, v_ref, tile)


def coarse_residual(lv, b_ref, w, v_ref, out_ref):
    def tile(y, r, v, total):
        at = (y, pl.ds(r, 8), slice(None))
        out_ref[at] = (b_ref[at] + total) - w[0][6, y, pl.ds(r, 8), :] * v

    coarse_apply(lv, w, v_ref, tile)


def coarse_fold(lv, next_lv, ref, out_ref, scale):
    lane = lane_iota()
    even = (lane // lv.step) % 2 == 0
    joined = lv.planes // next_lv.planes

    def plane(i):
        for r in next_lv.tiles:
            base = ROW0 + 2 * (r - ROW0)
            total = None
            for j in range(joined):
                for c in range(2):
                    value = ref[1 + joined * i + j, pl.ds(base + c, 8, stride=2), :]
                    total = value if total is None else total + value
            if lv.split:
                total = total + roll(total, LANES // 2)
            other = jnp.where(even, roll(total, -lv.step), roll(total, lv.step))
            out_ref[1 + i, pl.ds(r, 8), :] = scale * (total + other)

    loop(next_lv.planes, 4, plane)


def coarse_correct(lv, next_lv, e_ref, s_ref, t_ref):
    joined = lv.planes // next_lv.planes

    def plane(i):
        for r in next_lv.tiles:
            e = e_ref[1 + i, pl.ds(r, 8), :]
            base = ROW0 + 2 * (r - ROW0)
            for j in range(joined):
                for c in range(2):
                    at = (1 + joined * i + j, pl.ds(base + c, 8, stride=2), slice(None))
                    t_ref[at] = s_ref[at] + e

    loop(next_lv.planes, 4, plane)


def zero_margin(lv, ref):
    zero = jnp.zeros((8, LANES), F32)
    for y in (0, lv.planes + 1):
        for r in lv.tiles:
            ref[y, pl.ds(r, 8), :] = zero

    def plane(y):
        ref[y, pl.ds(0, 8), :] = zero
        ref[y, pl.ds(ROW0 + lv.n, 8), :] = zero

    loop(lv.planes + 2, 1, plane)


class Links:
    def __init__(self, send, recv):
        self.send, self.recv, self.used = send, recv, 0

    def copy(self, src, dst, device):
        index = self.used
        self.used += 1
        return pltpu.make_async_remote_copy(
            src_ref=src,
            dst_ref=dst,
            send_sem=self.send.at[index],
            recv_sem=self.recv.at[index],
            device_id=device,
            device_id_type=MESH,
        )


class Halo:
    def __init__(self, place, links, sources, targets):
        self.place = place
        gx, gy = place[0], place[1]
        self.copies = [
            (d, links.copy(sources[d], targets[d], (gx + d[0], gy + d[1]))) for d in NEIGHBOURS
        ]

    def start(self):
        for (dx, dy), copy in self.copies:
            pl.when(there(self.place, dx, dy))(copy.start)

    def wait_recv(self):
        for (dx, dy), copy in self.copies:
            pl.when(there(self.place, -dx, -dy))(copy.wait_recv)

    def wait_send(self):
        for (dx, dy), copy in self.copies:
            pl.when(there(self.place, dx, dy))(copy.wait_send)


def there(place, dx, dy):
    gx, gy, nx, ny = place
    ok = None
    for at, by, size in ((gx, dx, nx), (gy, dy, ny)):
        if by:
            test = at + by < size if by > 0 else at + by >= 0
            ok = test if ok is None else jnp.logical_and(ok, test)
    return True if ok is None else ok


class Rim:
    def __init__(self, lv, halo, refs):
        self.lv, self.halo = lv, halo
        self.send_x, self.send_y, self.recv_x, self.recv_y = refs

    @staticmethod
    def scratch(lv, halo):
        n, parts = lv.n, lv.parts
        return [
            pltpu.VMEM((2, parts, halo, n, LANES), F32),
            pltpu.VMEM((2, parts, n, halo, LANES), F32),
            pltpu.VMEM((2, parts, halo, n, LANES), F32),
            pltpu.VMEM((2, parts, n + 2 * halo, halo, LANES), F32),
        ]

    def pack(self, ref):
        lv, h = self.lv, self.halo
        for side, start in ((0, lv.off), (1, lv.off + lv.n - h)):
            for p in range(lv.parts):
                for i in range(h):
                    self.send_x[side, p, i] = ref[p, start + i, pl.ds(ROW0, lv.n), :]

        def plane(i):
            for p in range(lv.parts):
                self.send_y[0, p, i] = ref[p, lv.off + i, pl.ds(ROW0, h), :]
                self.send_y[1, p, i] = ref[p, lv.off + i, pl.ds(ROW0 + lv.n - h, h), :]

        loop(lv.n, 2, plane)

    def exchange(self, place, links):
        lv, h, n = self.lv, self.halo, self.lv.n
        sources, targets = {}, {}
        for dx, dy in NEIGHBOURS:
            if dy == 0:
                sources[dx, dy] = self.send_x.at[1 if dx > 0 else 0]
                targets[dx, dy] = self.recv_x.at[0 if dx > 0 else 1]
            else:
                src = self.send_y.at[1 if dy > 0 else 0]
                dst = self.recv_y.at[0 if dy > 0 else 1]
                if dx == 0:
                    sources[dx, dy] = src
                    targets[dx, dy] = dst.at[:, h : h + n]
                elif dx > 0:
                    sources[dx, dy] = src.at[:, n - h : n]
                    targets[dx, dy] = dst.at[:, 0:h]
                else:
                    sources[dx, dy] = src.at[:, 0:h]
                    targets[dx, dy] = dst.at[:, h + n : n + 2 * h]
        return Halo(place, links, sources, targets)

    def unpack(self, ref, place):
        lv, h, n = self.lv, self.halo, self.lv.n
        for side, start, dx in ((0, lv.off - h, -1), (1, lv.off + n, 1)):
            ok = there(place, dx, 0)
            for p in range(lv.parts):
                for i in range(h):
                    value = self.recv_x[side, p, i]
                    ref[p, start + i, pl.ds(ROW0, n), :] = jnp.where(ok, value, 0.0)

        gx, gy, nx, ny = place

        def plane(i):
            cell = gx * n + (i - h)
            in_x = jnp.logical_and(cell >= 0, cell < nx * n)
            for side, row, dy in ((0, ROW0 - h, -1), (1, ROW0 + n, 1)):
                ok = jnp.logical_and(in_x, there(place, 0, dy))
                for p in range(lv.parts):
                    value = self.recv_y[side, p, i]
                    ref[p, lv.off - h + i, pl.ds(row, h), :] = jnp.where(ok, value, 0.0)

        loop(n + 2 * h, 2, plane)


class Blocks:
    def __init__(self, lv, refs):
        self.lv = lv
        self.send, self.recv = refs

    @staticmethod
    def scratch(lv):
        n = lv.n
        return [pltpu.VMEM((n, n, LANES), F32), pltpu.VMEM((3, 3 * n, n, LANES), F32)]

    def pack(self, ref):
        lv = self.lv
        for i in range(lv.n):
            self.send[i] = ref[0, lv.off + i, pl.ds(ROW0, lv.n), :]

    def exchange(self, place, links):
        n = self.lv.n
        sources = {d: self.send for d in NEIGHBOURS}
        targets = {
            (dx, dy): self.recv.at[1 - dy, n * (1 - dx) : n * (1 - dx) + n] for dx, dy in NEIGHBOURS
        }
        return Halo(place, links, sources, targets)

    def unpack(self, ref, place):
        lv, n = self.lv, self.lv.n
        for j in range(3):
            for i in range(3):
                if (i, j) == (1, 1):
                    continue
                ok = there(place, i - 1, j - 1)
                for k in range(n):
                    value = self.recv[j, n * i + k]
                    ref[0, lv.off + n * (i - 1) + k, pl.ds(ROW0 + n * (j - 1), n), :] = jnp.where(
                        ok, value, 0.0
                    )


class Gather:
    def __init__(self, place, links, piece_ref, whole_ref):
        gx, gy, nx, ny = place
        self.place = place
        self.piece, self.whole = piece_ref, whole_ref
        mine = piece_ref.at[gx]
        self.along_x = [
            links.copy(mine, mine, (lax.rem(gx + d, nx), gy)) for d in range(1, nx)
        ]
        slab = whole_ref.at[1 + gy, pl.ds(ROW0, 2 * nx), :]
        self.along_y = [
            links.copy(slab, slab, (gx, lax.rem(gy + d, ny))) for d in range(1, ny)
        ]

    def start_x(self, value):
        gx = self.place[0]
        self.piece[gx] = value
        for copy in self.along_x:
            copy.start()

    def start_y(self):
        gx, gy, nx, ny = self.place
        for copy in self.along_x:
            copy.wait_recv()
        for i in range(nx):
            self.whole[1 + gy, pl.ds(ROW0 + 2 * i, 2), :] = self.piece[i]
        for copy in self.along_y:
            copy.start()

    def finish(self):
        for copy in self.along_y:
            copy.wait_recv()

    def wait_send(self):
        for copy in self.along_x + self.along_y:
            copy.wait_send()


def scratch_shapes(nx, ny):
    l3, l4, l5 = coarse_levels(nx, ny)
    shapes = {}
    for name in ("raw_k", "raw_b", "out"):
        shapes[name] = pltpu.VMEM((L0.n, L0.n, L0.parts * LANES), F32)
    shapes["perm"] = pltpu.VMEM((512, 512), BF16)
    shapes["back"] = pltpu.VMEM((512, 512), BF16)
    shapes["left"] = pltpu.VMEM((8, 2 * LANES), F32)
    for i, lv in enumerate((L0, L1, L2)):
        for name in ("k", "b", "wx", "wy", "inv", "diag", "x", "s", "t"):
            shapes[name + str(i)] = pltpu.VMEM(lv.shape, F32)
        shapes["wz" + str(i)] = pltpu.VMEM((lv.parts + 1,) + lv.shape[1:], F32)
        shapes["tmp" + str(i)] = pltpu.VMEM((max(lv.parts // 2, 1), lv.n // 2, max(lv.n, 8), LANES), F32)
    shapes["e2"] = pltpu.VMEM((6, L2.rows, LANES), F32)
    for i, lv in ((3, l3), (4, l4), (5, l5)):
        for name in ("k", "b", "x", "s", "t"):
            shapes[name + str(i)] = pltpu.VMEM(lv.shape, F32)
        shapes["w" + str(i)] = pltpu.VMEM((8,) + lv.shape, F32)
    for name, lv, halo in (("rk0", L0, 3), ("rb0", L0, 2), ("rs0", L0, 2), ("rk1", L1, 5), ("rb1", L1, 4)):
        for j, shape in enumerate(Rim.scratch(lv, halo)):
            shapes[name + "_" + str(j)] = shape
    for name in ("rk2", "rb2", "rs2"):
        for j, shape in enumerate(Blocks.scratch(L2)):
            shapes[name + "_" + str(j)] = shape
    for name in ("pk3", "pb3"):
        shapes[name] = pltpu.VMEM((nx, 2, LANES), F32)
    copies = 8 * 8 + 2 * (nx - 1 + ny - 1)
    shapes["send"] = pltpu.SemaphoreType.DMA((copies,))
    shapes["recv"] = pltpu.SemaphoreType.DMA((copies,))
    shapes["local"] = pltpu.SemaphoreType.DMA((3,))
    return shapes


def coarse_levels(nx, ny):
    return (
        Coarse(ny, 2 * nx, 1, True),
        Coarse(ny, nx, 2, False),
        Coarse(ny // 2, nx // 2, 4, False),
    )


def kernel(nx, ny, names, b_in, k_in, out_ref, *refs):
    m = dict(zip(names, refs))
    gx, gy = lax.axis_index("gx"), lax.axis_index("gy")
    place = (gx, gy, nx, ny)
    l3, l4, l5 = coarse_levels(nx, ny)
    links = Links(m["send"], m["recv"])

    def pair(name, cls, *args):
        refs = [m[key] for key in names if key.startswith(name + "_")]
        return cls(*args, refs)

    rk0, rb0, rs0 = (pair(name, Rim, L0, h) for name, h in (("rk0", 3), ("rb0", 2), ("rs0", 2)))
    rk1, rb1 = (pair(name, Rim, L1, h) for name, h in (("rk1", 5), ("rb1", 4)))
    rk2, rb2, rs2 = (pair(name, Blocks, L2) for name in ("rk2", "rb2", "rs2"))
    hk0, hb0, hs0, hk1, hb1, hk2, hb2, hs2 = (
        rim.exchange(place, links) for rim in (rk0, rb0, rs0, rk1, rb1, rk2, rb2, rs2)
    )
    gk3 = Gather(place, links, m["pk3"], m["k3"])
    gb3 = Gather(place, links, m["pb3"], m["b3"])

    load_k = pltpu.make_async_copy(k_in, m["raw_k"], m["local"].at[0])
    load_b = pltpu.make_async_copy(b_in, m["raw_b"], m["local"].at[1])
    load_k.start()
    load_b.start()

    barrier = pltpu.get_barrier_semaphore()
    for d in range(1, nx):
        pl.semaphore_signal(
            barrier, inc=1, device_id=(lax.rem(gx + d, nx), gy), device_id_type=MESH
        )
    for d in range(1, ny):
        pl.semaphore_signal(
            barrier, inc=1, device_id=(gx, lax.rem(gy + d, ny)), device_id_type=MESH
        )
    corners = [d for d in NEIGHBOURS if d[0] and d[1]]
    for dx, dy in corners:

        @pl.when(there(place, dx, dy))
        def _():
            pl.semaphore_signal(
                barrier, inc=1, device_id=(gx + dx, gy + dy), device_id_type=MESH
            )

    def one(rows, cols, test):
        at = lax.broadcasted_iota(jnp.int32, (rows, cols), 0)
        to = lax.broadcasted_iota(jnp.int32, (rows, cols), 1)
        return jnp.where(test(at, to), 1.0, 0.0).astype(BF16)

    def fill(i):
        start = pl.multiple_of(i * 64, 64)
        m["perm"][pl.ds(start, 64), :] = one(
            64, 512, lambda at, to: at + start == 4 * (to % LANES) + to // LANES
        )
        m["back"][pl.ds(start, 64), :] = one(
            64, 512, lambda at, to: to == 4 * ((at + start) % LANES) + (at + start) // LANES
        )

    loop(8, 1, fill)
    m["left"][...] = jnp.zeros_like(m["left"])
    fold = one(
        2 * LANES,
        LANES,
        lambda at, to: jnp.logical_and(at // LANES == to // 64, (at % LANES) // 2 == to % 64),
    )
    unfold = one(
        LANES,
        2 * LANES,
        lambda at, to: jnp.logical_and(to // LANES == at // 64, (to % LANES) // 2 == at % 64),
    )

    def reorder(raw, ref):
        half = L0.n // 2
        for c in range(2):
            value = raw[c * half : (c + 1) * half].reshape(half * L0.n, 512)
            moved = exact_dot(value, m["perm"][...])
            for p in range(L0.parts):
                ref[p, pl.ds(L0.off + c * half, half), pl.ds(ROW0, L0.n), :] = moved[
                    :, p * LANES : (p + 1) * LANES
                ].reshape(half, L0.n, LANES)

    load_k.wait()
    reorder(m["raw_k"], m["k0"])
    rk0.pack(m["k0"])
    beside_x = jnp.where(gx > 0, 1, 0) + jnp.where(gx < nx - 1, 1, 0)
    beside_y = jnp.where(gy > 0, 1, 0) + jnp.where(gy < ny - 1, 1, 0)
    pl.semaphore_wait(barrier, nx - 1 + ny - 1 + beside_x * beside_y)
    hk0.start()
    load_b.wait()
    reorder(m["raw_b"], m["b0"])
    rb0.pack(m["b0"])
    hb0.start()

    fold_x(L0, m["k0"], m["tmp0"])
    fold_y(L0, m["tmp0"], m["k1"], L1.off, 0.125)
    rk1.pack(m["k1"])
    hk1.start()
    fold_x(L1, m["k1"], m["tmp1"])
    fold_y(L1, m["tmp1"], m["k2"], L2.off, 0.125)
    rk2.pack(m["k2"])
    hk2.start()
    fold_x(L2, m["k2"], m["tmp2"])
    gk3.start_x(fold_z(m["tmp2"], m["left"], fold, 0.125)[0:2])
    for lv, i in ((l3, 3), (l4, 4), (l5, 5)):
        for name in ("k", "x", "s", "t"):
            zero_margin(lv, m[name + str(i)])

    weights = [
        tuple(m[name + str(i)] for name in ("wx", "wy", "wz", "inv", "diag")) for i in range(3)
    ]
    sizes = [(nx * lv.n, ny * lv.n) for lv in (L0, L1, L2)]
    w3, w4, w5 = (m["w3"],), (m["w4"],), (m["w5"],)

    hk0.wait_recv()
    rk0.unpack(m["k0"], place)
    fine_setup(L0, m["k0"], weights[0], gx, gy, *sizes[0])
    hb0.wait_recv()
    rb0.unpack(m["b0"], place)
    fine_first(L0, m["b0"], weights[0], m["x0"], 2)
    fine_step(L0, m["b0"], weights[0], m["x0"], None, m["s0"], 1, KEEP, OLD, STEP)
    fine_restrict(L0, m["b0"], weights[0], m["s0"], m["tmp0"])
    fold_y(L0, m["tmp0"], m["b1"], L1.off, 0.5)
    rb1.pack(m["b1"])
    hb1.start()
    rs0.pack(m["s0"])
    hs0.start()

    gk3.start_y()
    hk1.wait_recv()
    rk1.unpack(m["k1"], place)
    fine_setup(L1, m["k1"], weights[1], gx, gy, *sizes[1])
    hb1.wait_recv()
    rb1.unpack(m["b1"], place)
    fine_first(L1, m["b1"], weights[1], m["x1"], 4)
    fine_step(L1, m["b1"], weights[1], m["x1"], None, m["s1"], 3, KEEP, OLD, STEP)
    fine_restrict(L1, m["b1"], weights[1], m["s1"], m["tmp1"])
    fold_y(L1, m["tmp1"], m["b2"], L2.off, 0.5)
    rb2.pack(m["b2"])
    hb2.start()

    hk2.wait_recv()
    rk2.unpack(m["k2"], place)
    fine_setup(L2, m["k2"], weights[2], gx, gy, *sizes[2])
    hb2.wait_recv()
    rb2.unpack(m["b2"], place)
    fine_first(L2, m["b2"], weights[2], m["x2"], 2)
    fine_step(L2, m["b2"], weights[2], m["x2"], None, m["s2"], 1, KEEP, OLD, STEP)
    fine_restrict(L2, m["b2"], weights[2], m["s2"], m["tmp2"])
    gb3.start_x(fold_z(m["tmp2"], m["left"], fold, 0.5)[0:2])
    rs2.pack(m["s2"])
    hs2.start()

    gk3.finish()
    coarse_setup(l3, m["k3"], w3)
    gb3.start_y()
    coarse_fold(l3, l4, m["k3"], m["k4"], 0.125)
    coarse_setup(l4, m["k4"], w4)
    coarse_fold(l4, l5, m["k4"], m["k5"], 0.125)
    coarse_setup(l5, m["k5"], w5)
    gb3.finish()

    coarse_first(l3, m["b3"], w3, m["x3"])
    coarse_step(l3, m["b3"], w3, m["x3"], None, m["s3"], KEEP, OLD, STEP)
    coarse_residual(l3, m["b3"], w3, m["s3"], m["t3"])
    coarse_fold(l3, l4, m["t3"], m["b4"], 0.5)
    coarse_first(l4, m["b4"], w4, m["x4"])
    coarse_step(l4, m["b4"], w4, m["x4"], None, m["s4"], KEEP, OLD, STEP)
    coarse_residual(l4, m["b4"], w4, m["s4"], m["t4"])
    coarse_fold(l4, l5, m["t4"], m["b5"], 0.5)
    coarse_first(l5, m["b5"], w5, m["x5"])
    now, old, spare = m["x5"], None, [m["s5"], m["t5"]]
    rho = RHO0
    for _ in range(COARSE_ITERS - 1):
        rho_new = 1.0 / (2.0 * SIGMA - rho)
        keep = 1.0 + rho_new * rho - 2.0 * rho_new / RADIUS
        out = spare.pop(0)
        coarse_step(l5, m["b5"], w5, now, old, out, keep, rho_new * rho, 2.0 * rho_new / RADIUS)
        if old is not None:
            spare.append(old)
        now, old, rho = out, now, rho_new
    coarse_correct(l4, l5, now, m["s4"], m["t4"])
    coarse_step(l4, m["b4"], w4, m["t4"], None, m["x4"], 1.0 - FIRST, 0.0, FIRST)
    coarse_step(l4, m["b4"], w4, m["x4"], m["t4"], m["s4"], KEEP, OLD, STEP)
    coarse_correct(l3, l4, m["s4"], m["s3"], m["t3"])
    coarse_step(l3, m["b3"], w3, m["t3"], None, m["x3"], 1.0 - FIRST, 0.0, FIRST)
    coarse_step(l3, m["b3"], w3, m["x3"], m["t3"], m["s3"], KEEP, OLD, STEP)

    near = jnp.concatenate(
        [m["s3"][gy + d, pl.ds(2 * gx + ROW0 - 2, 8), :] for d in range(3)], axis=0
    )
    wide = exact_dot(near, unfold)
    for d in range(3):
        for i in range(6):
            for a in range(2):
                row = wide[8 * d + i : 8 * d + i + 1, a * LANES : (a + 1) * LANES]
                m["e2"][i, pl.ds(ROW0 - 4 + 4 * d + 2 * a, 2), :] = jnp.broadcast_to(
                    row, (2, LANES)
                )
    hs2.wait_recv()
    hs2.wait_send()
    rs2.unpack(m["s2"], place)
    for i in range(6):
        for k in range(2):
            x = L2.off - 4 + 2 * i + k
            for r in L2.tiles(4):
                m["t2"][0, x, pl.ds(r, 8), :] = (
                    m["s2"][0, x, pl.ds(r, 8), :] + m["e2"][i, pl.ds(r, 8), :]
                )
    fine_step(L2, m["b2"], weights[2], m["t2"], None, m["x2"], 3, 1.0 - FIRST, 0.0, FIRST)
    fine_step(L2, m["b2"], weights[2], m["x2"], m["t2"], m["s2"], 2, KEEP, OLD, STEP)

    fine_correct(L1, L2, m["s2"], m["s1"], m["t1"], 3)
    fine_step(L1, m["b1"], weights[1], m["t1"], None, m["x1"], 2, 1.0 - FIRST, 0.0, FIRST)
    fine_step(L1, m["b1"], weights[1], m["x1"], m["t1"], m["s1"], 1, KEEP, OLD, STEP)

    hs0.wait_recv()
    hs0.wait_send()
    rs0.unpack(m["s0"], place)
    fine_correct(L0, L1, m["s1"], m["s0"], m["t0"], 2)
    fine_step(L0, m["b0"], weights[0], m["t0"], None, m["x0"], 1, 1.0 - FIRST, 0.0, FIRST)
    fine_step(L0, m["b0"], weights[0], m["x0"], m["t0"], m["s0"], 0, KEEP, OLD, STEP)

    half = L0.n // 2
    for c in range(2):
        value = jnp.concatenate(
            [
                m["s0"][p, pl.ds(L0.off + c * half, half), pl.ds(ROW0, L0.n), :].reshape(
                    half * L0.n, LANES
                )
                for p in range(L0.parts)
            ],
            axis=1,
        )
        moved = exact_dot(value, m["back"][...])
        m["out"][c * half : (c + 1) * half] = moved.reshape(half, L0.n, 512)
    store = pltpu.make_async_copy(m["out"], out_ref, m["local"].at[2])
    store.start()
    for part in (hk0, hb0, hk1, hb1, hk2, hb2, gk3, gb3):
        part.wait_send()
    store.wait()


def solution(mesh):
    nx, ny = mesh.shape["gx"], mesh.shape["gy"]
    shapes = scratch_shapes(nx, ny)

    def body(right_side, coefficient):
        return pl.pallas_call(
            functools.partial(kernel, nx, ny, list(shapes)),
            out_shape=jax.ShapeDtypeStruct(right_side.shape, F32),
            in_specs=[pl.BlockSpec(memory_space=pl.ANY)] * 2,
            out_specs=pl.BlockSpec(memory_space=pl.ANY),
            scratch_shapes=list(shapes.values()),
            compiler_params=pltpu.CompilerParams(
                collective_id=0, has_side_effects=True, vmem_limit_bytes=56 * 1024 * 1024
            ),
        )(right_side, coefficient)

    return jax.shard_map(
        body,
        mesh=mesh,
        in_specs=(P("gx", "gy", None), P("gx", "gy", None)),
        out_specs=P("gx", "gy", None),
        check_vma=False,
    )
```

time: 791 us -> 58.2 us (0.07)
  the two profiles are of different devices: /device:TPU:119 before, /device:TPU:1 now
where the time goes in v1:
time: 58.2 us; the launch traced here: 58 us
  Pallas kernels  56.1 us (96%)
  local copies, waits for them, and re-layouts  1.88 us (3%)
    pallas_call x1, Pallas kernels, body(): pl.pallas_call(functools.partial(kernel, nx, ny, list(shapes)), out_shape...  56.1 us
    unnamed x1, local copies, waits for them, and re-layouts  1.88 us

profile of v1, /device:TPU:1, one launch (start us, length us, event | category | flops | bytes accessed | tf_op | source)
XLA Modules:
  0.0 58.0 jit_solution(12033095955247364125)
XLA Ops:
  0.0 56.1 %shard_map.28 = f32[16,16,512]{2,1,0:T(8,128)} custom-call(f32[16,16,512]{2,1,0:T(8,128)} %b_in.1, f32[16,16,512]{2,1,0:T(8,128)} %k_in.1), custom_call_target="tpu_custom_call" | custom-call | tf_op jit(solution)/shard_map/pallas_call | solution.py:885
  56.1 1.9 %copy.4 = f32[16,16,512]{2,1,0:T(8,128)} copy(f32[16,16,512]{2,1,0:T(8,128)} %shard_map.28) | data formatting | bytes 1048576

commit v2 on v1

--- a/solution.py
+++ b/solution.py
@@ -40,7 +40,7 @@
         if count % 8 == 0:
             return [low + 8 * t for t in range(count // 8)]
         tiles = -(-count // 8)
-        low -= (tiles * 8 - count) // 2
+        low = max(1, low - (tiles * 8 - count) // 2)
         return [low + 8 * t for t in range(tiles)]
 
 
@@ -52,7 +52,7 @@
 
 
 L0 = Fine(4, 16, 4, 32, 2)
-L1 = Fine(2, 8, 6, 24, 4)
+L1 = Fine(2, 8, 8, 32, 6)
 L2 = Fine(1, 4, 5, 24, 3)
 
 
@@ -73,6 +73,10 @@
         return carry
 
     lax.fori_loop(0, count // step, turn, 0)
+
+
+def turns(count, most):
+    return max(d for d in range(1, most + 1) if count % d == 0)
 
 
 def split3(value):
@@ -91,117 +95,158 @@
     return total
 
 
+class Batch:
+    def __init__(self):
+        self.seen, self.held = {}, []
+
+    def get(self, ref, p, x, dx, r):
+        key = (id(ref), p, dx, r)
+        if key not in self.seen:
+            self.seen[key] = ref[p, x + dx, pl.ds(r, 8), :]
+        return self.seen[key]
+
+    def put(self, ref, p, x, dx, r, value):
+        self.held.append((ref, p, x, dx, r, value))
+
+    def flush(self):
+        for ref, p, x, dx, r, value in self.held:
+            ref[p, x + dx, pl.ds(r, 8), :] = value
+        self.held = []
+
+
 def fine_setup(lv, k_ref, w, gx, gy, size_x, size_y):
     wx, wy, wz, inv, diag = w
     h = lv.halo_inv
     lane = lane_iota()
     row = lax.broadcasted_iota(jnp.int32, (8, LANES), 0)
     parts = lv.parts
-
-    def plane(i):
-        x = lv.off - h + i
-        gx_cell = gx * lv.n + (i - h)
-        in_x = jnp.logical_and(gx_cell >= 0, gx_cell < size_x)
+    count = lv.n + 2 * h + 1
+    width = turns(count, 12 // parts)
+
+    def planes(i):
+        x = lv.off - h + width * i
         for r in lv.tiles(h):
-            cells = [k_ref[p, x, pl.ds(r, 8), :] for p in range(parts)]
+            now = Batch()
             gy_cell = gy * lv.n + (r - ROW0) + row
-            inside = jnp.logical_and(jnp.logical_and(gy_cell >= 0, gy_cell < size_y), in_x)
-            first = jnp.where(lane == 0, 0.0, roll(cells[parts - 1], 1))
-            last = jnp.where(lane == LANES - 1, 0.0, roll(cells[0], -1))
-            for p in range(parts):
-                k = cells[p]
-                kxm = k_ref[p, x - 1, pl.ds(r, 8), :]
-                kxp = k_ref[p, x + 1, pl.ds(r, 8), :]
-                kym = k_ref[p, x, pl.ds(r - 1, 8), :]
-                kyp = k_ref[p, x, pl.ds(r + 1, 8), :]
-                kzm = first if p == 0 else cells[p - 1]
-                kzp = last if p == parts - 1 else cells[p + 1]
-                wx[p, x, pl.ds(r, 8), :] = 0.5 * (k + kxm)
-                wy[p, x, pl.ds(r, 8), :] = 0.5 * (k + kym)
-                down = 0.5 * (k + kzm)
-                if p == 0:
-                    down = jnp.where(lane == 0, 0.0, down)
-                    wz[parts, x, pl.ds(r, 8), :] = roll(down, -1)
-                wz[p, x, pl.ds(r, 8), :] = down
-                d = 3.0 * k + 0.5 * (((kxm + kxp) + (kym + kyp)) + (kzm + kzp))
-                diag[p, x, pl.ds(r, 8), :] = d
-                inv[p, x, pl.ds(r, 8), :] = jnp.where(inside, 1.0 / d, 0.0)
-
-    count = lv.n + 2 * h + 1
-    loop(count, 1, plane)
-
-
-def fine_sum(lv, v_ref, w, x, r):
+            in_y = jnp.logical_and(gy_cell >= 0, gy_cell < size_y)
+            cells = [[now.get(k_ref, p, x, j, r) for p in range(parts)] for j in range(width)]
+            below = [roll(c[parts - 1], 1) for c in cells]
+            above = [roll(c[0], -1) for c in cells]
+            for j in range(width):
+                gx_cell = gx * lv.n + (width * i + j - h)
+                inside = jnp.logical_and(in_y, jnp.logical_and(gx_cell >= 0, gx_cell < size_x))
+                first = jnp.where(lane == 0, 0.0, below[j])
+                last = jnp.where(lane == LANES - 1, 0.0, above[j])
+                for p in range(parts):
+                    k = cells[j][p]
+                    kxm, kxp = now.get(k_ref, p, x, j - 1, r), now.get(k_ref, p, x, j + 1, r)
+                    kym, kyp = now.get(k_ref, p, x, j, r - 1), now.get(k_ref, p, x, j, r + 1)
+                    kzm = first if p == 0 else cells[j][p - 1]
+                    kzp = last if p == parts - 1 else cells[j][p + 1]
+                    now.put(wx, p, x, j, r, 0.5 * (k + kxm))
+                    now.put(wy, p, x, j, r, 0.5 * (k + kym))
+                    down = 0.5 * (k + kzm)
+                    if p == 0:
+                        down = jnp.where(lane == 0, 0.0, down)
+                    now.put(wz, p, x, j, r, down)
+                    if p == parts - 1:
+                        up = jnp.where(lane == LANES - 1, 0.0, 0.5 * (k + kzp))
+                        now.put(wz, parts, x, j, r, up)
+                    d = 3.0 * k + 0.5 * (((kxm + kxp) + (kym + kyp)) + (kzm + kzp))
+                    now.put(diag, p, x, j, r, d)
+                    now.put(inv, p, x, j, r, jnp.where(inside, 1.0 / d, 0.0))
+            now.flush()
+
+    loop(count // width, 1, planes)
+
+
+def fine_sum(lv, now, v_ref, w, x, width, r):
     wx, wy, wz = w[0], w[1], w[2]
     parts = lv.parts
-    cells = [v_ref[p, x, pl.ds(r, 8), :] for p in range(parts)]
-    below, above = roll(cells[parts - 1], 1), roll(cells[0], -1)
+    cells = [[now.get(v_ref, p, x, j, r) for p in range(parts)] for j in range(width)]
+    below = [roll(c[parts - 1], 1) for c in cells]
+    above = [roll(c[0], -1) for c in cells]
     sums = []
-    for p in range(parts):
-        along_x = (
-            wx[p, x, pl.ds(r, 8), :] * v_ref[p, x - 1, pl.ds(r, 8), :]
-            + wx[p, x + 1, pl.ds(r, 8), :] * v_ref[p, x + 1, pl.ds(r, 8), :]
-        )
-        along_y = (
-            wy[p, x, pl.ds(r, 8), :] * v_ref[p, x, pl.ds(r - 1, 8), :]
-            + wy[p, x, pl.ds(r + 1, 8), :] * v_ref[p, x, pl.ds(r + 1, 8), :]
-        )
-        along_z = wz[p, x, pl.ds(r, 8), :] * (below if p == 0 else cells[p - 1]) + wz[
-            p + 1, x, pl.ds(r, 8), :
-        ] * (above if p == parts - 1 else cells[p + 1])
-        sums.append((along_x + along_y) + along_z)
+    for j in range(width):
+        sums.append([])
+        for p in range(parts):
+            along_x = now.get(wx, p, x, j, r) * now.get(v_ref, p, x, j - 1, r) + now.get(
+                wx, p, x, j + 1, r
+            ) * now.get(v_ref, p, x, j + 1, r)
+            along_y = now.get(wy, p, x, j, r) * now.get(v_ref, p, x, j, r - 1) + now.get(
+                wy, p, x, j, r + 1
+            ) * now.get(v_ref, p, x, j, r + 1)
+            along_z = now.get(wz, p, x, j, r) * (below[j] if p == 0 else cells[j][p - 1])
+            along_z += now.get(wz, p + 1, x, j, r) * (
+                above[j] if p == parts - 1 else cells[j][p + 1]
+            )
+            sums[j].append((along_x + along_y) + along_z)
     return sums, cells
 
 
 def fine_first(lv, b_ref, w, out_ref, halo):
     inv = w[3]
 
-    def plane(i):
-        x = lv.off - halo + i
+    def planes(i):
+        x = lv.off - halo + 2 * i
+        now = Batch()
         for r in lv.tiles(halo):
-            for p in range(lv.parts):
-                at = (p, x, pl.ds(r, 8), slice(None))
-                out_ref[at] = FIRST * (inv[at] * b_ref[at])
-
-    loop(lv.n + 2 * halo, 2, plane)
+            for k in range(2):
+                for p in range(lv.parts):
+                    value = now.get(inv, p, x, k, r) * now.get(b_ref, p, x, k, r)
+                    now.put(out_ref, p, x, k, r, FIRST * value)
+        now.flush()
+
+    loop((lv.n + 2 * halo) // 2, 1, planes)
 
 
 def fine_step(lv, b_ref, w, v_ref, old_ref, out_ref, halo, keep, old, step):
     inv = w[3]
-
-    def plane(i):
-        x = lv.off - halo + i
+    count = lv.n + 2 * halo
+    width = turns(count, 8 // lv.parts)
+
+    def planes(i):
+        x = lv.off - halo + width * i
         for r in lv.tiles(halo):
-            sums, cells = fine_sum(lv, v_ref, w, x, r)
-            for p in range(lv.parts):
-                at = (p, x, pl.ds(r, 8), slice(None))
-                value = keep * cells[p] + step * (inv[at] * (b_ref[at] + sums[p]))
-                if old_ref is not None:
-                    value = value - old * old_ref[at]
-                out_ref[at] = value
-
-    loop(lv.n + 2 * halo, 2, plane)
-
-
-def fine_restrict(lv, b_ref, w, v_ref, tmp_ref):
+            now = Batch()
+            sums, cells = fine_sum(lv, now, v_ref, w, x, width, r)
+            for j in range(width):
+                for p in range(lv.parts):
+                    value = keep * cells[j][p] + step * (
+                        now.get(inv, p, x, j, r) * (now.get(b_ref, p, x, j, r) + sums[j][p])
+                    )
+                    if old_ref is not None:
+                        value = value - old * now.get(old_ref, p, x, j, r)
+                    now.put(out_ref, p, x, j, r, value)
+            now.flush()
+
+    loop(count // width, 1, planes)
+
+
+def fine_restrict(lv, b_ref, w, v_ref, tmp_ref, halo=0):
     diag = w[4]
     parts = lv.parts
-
-    def pair(i):
-        for r in lv.tiles(0):
-            total = [None] * max(parts // 2, 1)
-            for k in range(2):
-                x = lv.off + 2 * i + k
-                sums, cells = fine_sum(lv, v_ref, w, x, r)
-                for p in range(parts):
-                    at = (p, x, pl.ds(r, 8), slice(None))
-                    res = (b_ref[at] + sums[p]) - diag[at] * cells[p]
-                    q = p // 2
-                    total[q] = res if total[q] is None else total[q] + res
-            for q, value in enumerate(total):
-                tmp_ref[q, i, pl.ds(r - ROW0, 8), :] = value
-
-    loop(lv.n // 2, 1, pair)
+    count = lv.n + 2 * halo
+    width = 2 * turns(count // 2, 4 // parts)
+
+    def planes(i):
+        x = lv.off - halo + width * i
+        for r in lv.tiles(halo):
+            now = Batch()
+            sums, cells = fine_sum(lv, now, v_ref, w, x, width, r)
+            for pair in range(width // 2):
+                total = [None] * max(parts // 2, 1)
+                for j in (2 * pair, 2 * pair + 1):
+                    for p in range(parts):
+                        res = (now.get(b_ref, p, x, j, r) + sums[j][p]) - now.get(
+                            diag, p, x, j, r
+                        ) * cells[j][p]
+                        q = p // 2
+                        total[q] = res if total[q] is None else total[q] + res
+                for q, value in enumerate(total):
+                    tmp_ref[q, width // 2 * i + pair, pl.ds(r - ROW0 + halo, 8), :] = value
+
+    loop(count // width, 1, planes)
 
 
 def fold_x(lv, k_ref, tmp_ref):
@@ -219,13 +264,16 @@
     loop(lv.n // 2, 1, pair)
 
 
-def fold_y(lv, tmp_ref, out_ref, off, scale):
-    half = lv.n // 2
+def fold_y(lv, tmp_ref, out_ref, off, scale, halo=0):
+    half = lv.n // 2 + halo
     for q in range(lv.parts // 2):
+        sums = []
         for i in range(half):
             even = tmp_ref[q, i, pl.ds(0, half, stride=2), :]
             odd = tmp_ref[q, i, pl.ds(1, half, stride=2), :]
-            out_ref[q, off + i, pl.ds(ROW0, half), :] = scale * (even + odd)
+            sums.append(scale * (even + odd))
+        for i in range(half):
+            out_ref[q, off - halo // 2 + i, pl.ds(ROW0 - halo // 2, half), :] = sums[i]
 
 
 def fold_z(tmp_ref, left_ref, matrix, scale):
@@ -250,12 +298,15 @@
             for r in starts:
                 e = e_ref[q, big, pl.ds(r, 8), :]
                 base = 2 * (r - ROW0) + ROW0
+                held = []
                 for p in (2 * q, 2 * q + 1):
                     for k in range(2):
                         x = lv.off + 2 * (i - next_halo) + k
                         for c in range(2):
                             at = (p, x, pl.ds(base + c, 8, stride=2), slice(None))
-                            t_ref[at] = s_ref[at] + e
+                            held.append((at, s_ref[at] + e))
+                for at, value in held:
+                    t_ref[at] = value
 
     loop(next_lv.n + 2 * next_halo, 1, plane)
 
@@ -284,7 +335,7 @@
 def coarse_setup(lv, k_ref, w):
     lane = lane_iota() % (LANES // 2)
     bottom, top = lane < lv.step, lane >= LANES // 2 - lv.step
-    group = 2
+    group = 4 if lv.split else 8
 
     def planes(i):
         first = 1 + group * i
@@ -307,17 +358,20 @@
     loop(lv.planes // group, 1, planes)
 
 
-def coarse_apply(lv, w, v_ref, fn, group=4):
+def coarse_apply(lv, w, v_ref, out_ref, fn):
+    group = 4 if lv.split else 8
+
     def planes(i):
         first = 1 + group * i
+        held = []
         for r in lv.tiles:
             for j, beside in enumerate(coarse_beside(lv, v_ref, first, group, r)):
                 y = first + j
-                total = None
-                for f in range(6):
-                    term = w[0][f, y, pl.ds(r, 8), :] * beside[1 + f]
-                    total = term if total is None else total + term
-                fn(y, r, beside[0], total)
+                terms = [w[0][f, y, pl.ds(r, 8), :] * beside[1 + f] for f in range(6)]
+                total = ((terms[0] + terms[1]) + (terms[2] + terms[3])) + (terms[4] + terms[5])
+                held.append((y, r, fn(y, r, beside[0], total)))
+        for y, r, value in held:
+            out_ref[y, pl.ds(r, 8), :] = value
 
     loop(lv.planes // group, 1, planes)
 
@@ -337,17 +391,17 @@
         value = keep * v + step * (w[0][7, y, pl.ds(r, 8), :] * (b_ref[at] + total))
         if old_ref is not None:
             value = value - old * old_ref[at]
-        out_ref[at] = value
-
-    coarse_apply(lv, w, v_ref, tile)
+        return value
+
+    coarse_apply(lv, w, v_ref, out_ref, tile)
 
 
 def coarse_residual(lv, b_ref, w, v_ref, out_ref):
     def tile(y, r, v, total):
         at = (y, pl.ds(r, 8), slice(None))
-        out_ref[at] = (b_ref[at] + total) - w[0][6, y, pl.ds(r, 8), :] * v
-
-    coarse_apply(lv, w, v_ref, tile)
+        return (b_ref[at] + total) - w[0][6, y, pl.ds(r, 8), :] * v
+
+    coarse_apply(lv, w, v_ref, out_ref, tile)
 
 
 def coarse_fold(lv, next_lv, ref, out_ref, scale):
@@ -355,20 +409,34 @@
     even = (lane // lv.step) % 2 == 0
     joined = lv.planes // next_lv.planes
 
-    def plane(i):
-        for r in next_lv.tiles:
-            base = ROW0 + 2 * (r - ROW0)
-            total = None
-            for j in range(joined):
-                for c in range(2):
-                    value = ref[1 + joined * i + j, pl.ds(base + c, 8, stride=2), :]
-                    total = value if total is None else total + value
-            if lv.split:
-                total = total + roll(total, LANES // 2)
-            other = jnp.where(even, roll(total, -lv.step), roll(total, lv.step))
-            out_ref[1 + i, pl.ds(r, 8), :] = scale * (total + other)
-
-    loop(next_lv.planes, 4, plane)
+    group = 8
+
+    def planes(i):
+        totals = []
+        for k in range(group):
+            for r in next_lv.tiles:
+                base = ROW0 + 2 * (r - ROW0)
+                y = 1 + joined * (group * i + k)
+                terms = [
+                    ref[y + j, pl.ds(base + c, 8, stride=2), :]
+                    for j in range(joined)
+                    for c in range(2)
+                ]
+                total = terms[0] + terms[1]
+                if joined == 2:
+                    total = total + (terms[2] + terms[3])
+                totals.append(total)
+        if lv.split:
+            totals = [total + roll(total, LANES // 2) for total in totals]
+        totals = [
+            scale * (total + jnp.where(even, roll(total, -lv.step), roll(total, lv.step)))
+            for total in totals
+        ]
+        for k in range(group):
+            for j, r in enumerate(next_lv.tiles):
+                out_ref[1 + group * i + k, pl.ds(r, 8), :] = totals[k * len(next_lv.tiles) + j]
+
+    loop(next_lv.planes // group, 1, planes)
 
 
 def coarse_correct(lv, next_lv, e_ref, s_ref, t_ref):
@@ -378,10 +446,13 @@
         for r in next_lv.tiles:
             e = e_ref[1 + i, pl.ds(r, 8), :]
             base = ROW0 + 2 * (r - ROW0)
+            held = []
             for j in range(joined):
                 for c in range(2):
                     at = (1 + joined * i + j, pl.ds(base + c, 8, stride=2), slice(None))
-                    t_ref[at] = s_ref[at] + e
+                    held.append((at, s_ref[at] + e))
+            for at, value in held:
+                t_ref[at] = value
 
     loop(next_lv.planes, 4, plane)
 
@@ -403,38 +474,45 @@
     def __init__(self, send, recv):
         self.send, self.recv, self.used = send, recv, 0
 
-    def copy(self, src, dst, device):
+    def group(self):
         index = self.used
         self.used += 1
-        return pltpu.make_async_remote_copy(
-            src_ref=src,
-            dst_ref=dst,
-            send_sem=self.send.at[index],
-            recv_sem=self.recv.at[index],
-            device_id=device,
-            device_id_type=MESH,
-        )
+
+        def copy(src, dst, device):
+            return pltpu.make_async_remote_copy(
+                src_ref=src,
+                dst_ref=dst,
+                send_sem=self.send.at[index],
+                recv_sem=self.recv.at[index],
+                device_id=device,
+                device_id_type=MESH,
+            )
+
+        return copy
 
 
 class Halo:
-    def __init__(self, place, links, sources, targets):
-        self.place = place
-        gx, gy = place[0], place[1]
-        self.copies = [
-            (d, links.copy(sources[d], targets[d], (gx + d[0], gy + d[1]))) for d in NEIGHBOURS
-        ]
+    def __init__(self, place, links, groups):
+        gx, gy, nx, ny = place
+        self.copies, self.waits = [], []
+        for copies, whole in groups:
+            copy = links.group()
+            for (dx, dy), src, dst in copies:
+                device = (lax.rem(gx + dx + nx, nx), lax.rem(gy + dy + ny, ny))
+                self.copies.append(copy(src, dst, device))
+            self.waits.append(copy(whole, whole, device))
 
     def start(self):
-        for (dx, dy), copy in self.copies:
-            pl.when(there(self.place, dx, dy))(copy.start)
+        for copy in self.copies:
+            copy.start()
 
     def wait_recv(self):
-        for (dx, dy), copy in self.copies:
-            pl.when(there(self.place, -dx, -dy))(copy.wait_recv)
+        for wait in self.waits:
+            wait.wait_recv()
 
     def wait_send(self):
-        for (dx, dy), copy in self.copies:
-            pl.when(there(self.place, dx, dy))(copy.wait_send)
+        for wait in self.waits:
+            wait.wait_send()
 
 
 def there(place, dx, dy):
@@ -477,25 +555,23 @@
         loop(lv.n, 2, plane)
 
     def exchange(self, place, links):
-        lv, h, n = self.lv, self.halo, self.lv.n
-        sources, targets = {}, {}
+        h, n = self.halo, self.lv.n
+        faces, others = [], []
         for dx, dy in NEIGHBOURS:
             if dy == 0:
-                sources[dx, dy] = self.send_x.at[1 if dx > 0 else 0]
-                targets[dx, dy] = self.recv_x.at[0 if dx > 0 else 1]
+                src = self.send_x.at[1 if dx > 0 else 0]
+                faces.append(((dx, dy), src, self.recv_x.at[0 if dx > 0 else 1]))
+                continue
+            src = self.send_y.at[1 if dy > 0 else 0]
+            dst = self.recv_y.at[0 if dy > 0 else 1]
+            if dx == 0:
+                dst = dst.at[:, h : h + n]
+            elif dx > 0:
+                src, dst = src.at[:, n - h : n], dst.at[:, 0:h]
             else:
-                src = self.send_y.at[1 if dy > 0 else 0]
-                dst = self.recv_y.at[0 if dy > 0 else 1]
-                if dx == 0:
-                    sources[dx, dy] = src
-                    targets[dx, dy] = dst.at[:, h : h + n]
-                elif dx > 0:
-                    sources[dx, dy] = src.at[:, n - h : n]
-                    targets[dx, dy] = dst.at[:, 0:h]
-                else:
-                    sources[dx, dy] = src.at[:, 0:h]
-                    targets[dx, dy] = dst.at[:, h + n : n + 2 * h]
-        return Halo(place, links, sources, targets)
+                src, dst = src.at[:, 0:h], dst.at[:, h + n : n + 2 * h]
+            others.append(((dx, dy), src, dst))
+        return Halo(place, links, [(others, self.recv_y), (faces, self.recv_x)])
 
     def unpack(self, ref, place):
         lv, h, n = self.lv, self.halo, self.lv.n
@@ -528,7 +604,7 @@
     @staticmethod
     def scratch(lv):
         n = lv.n
-        return [pltpu.VMEM((n, n, LANES), F32), pltpu.VMEM((3, 3 * n, n, LANES), F32)]
+        return [pltpu.VMEM((n, n, LANES), F32), pltpu.VMEM((8, n, n, LANES), F32)]
 
     def pack(self, ref):
         lv = self.lv
@@ -537,24 +613,23 @@
 
     def exchange(self, place, links):
         n = self.lv.n
-        sources = {d: self.send for d in NEIGHBOURS}
-        targets = {
-            (dx, dy): self.recv.at[1 - dy, n * (1 - dx) : n * (1 - dx) + n] for dx, dy in NEIGHBOURS
-        }
-        return Halo(place, links, sources, targets)
+        copies = []
+        for dx, dy in NEIGHBOURS:
+            slot = (1 + dy) * 3 + 1 + dx
+            slot -= 1 if slot > 4 else 0
+            copies.append(((dx, dy), self.send, self.recv.at[slot]))
+        return Halo(place, links, [(copies, self.recv)])
 
     def unpack(self, ref, place):
         lv, n = self.lv, self.lv.n
-        for j in range(3):
-            for i in range(3):
-                if (i, j) == (1, 1):
-                    continue
-                ok = there(place, i - 1, j - 1)
-                for k in range(n):
-                    value = self.recv[j, n * i + k]
-                    ref[0, lv.off + n * (i - 1) + k, pl.ds(ROW0 + n * (j - 1), n), :] = jnp.where(
-                        ok, value, 0.0
-                    )
+        for dx, dy in NEIGHBOURS:
+            slot = (1 + dy) * 3 + 1 + dx
+            slot -= 1 if slot > 4 else 0
+            ok = there(place, -dx, -dy)
+            for k in range(n):
+                ref[0, lv.off - n * dx + k, pl.ds(ROW0 - n * dy, n), :] = jnp.where(
+                    ok, self.recv[slot, k], 0.0
+                )
 
 
 class Gather:
@@ -563,13 +638,15 @@
         self.place = place
         self.piece, self.whole = piece_ref, whole_ref
         mine = piece_ref.at[gx]
-        self.along_x = [
-            links.copy(mine, mine, (lax.rem(gx + d, nx), gy)) for d in range(1, nx)
-        ]
+        copy = links.group()
+        self.along_x = [copy(mine, mine, (lax.rem(gx + d, nx), gy)) for d in range(1, nx)]
+        rest = piece_ref.at[0 : nx - 1]
+        self.wait_x = copy(rest, rest, (lax.rem(gx + 1, nx), gy))
         slab = whole_ref.at[1 + gy, pl.ds(ROW0, 2 * nx), :]
-        self.along_y = [
-            links.copy(slab, slab, (gx, lax.rem(gy + d, ny))) for d in range(1, ny)
-        ]
+        copy = links.group()
+        self.along_y = [copy(slab, slab, (gx, lax.rem(gy + d, ny))) for d in range(1, ny)]
+        rest = whole_ref.at[1:ny, pl.ds(ROW0, 2 * nx), :]
+        self.wait_y = copy(rest, rest, (gx, lax.rem(gy + 1, ny)))
 
     def start_x(self, value):
         gx = self.place[0]
@@ -579,20 +656,18 @@
 
     def start_y(self):
         gx, gy, nx, ny = self.place
-        for copy in self.along_x:
-            copy.wait_recv()
+        self.wait_x.wait_recv()
         for i in range(nx):
             self.whole[1 + gy, pl.ds(ROW0 + 2 * i, 2), :] = self.piece[i]
         for copy in self.along_y:
             copy.start()
 
     def finish(self):
-        for copy in self.along_y:
-            copy.wait_recv()
+        self.wait_y.wait_recv()
 
     def wait_send(self):
-        for copy in self.along_x + self.along_y:
-            copy.wait_send()
+        self.wait_x.wait_send()
+        self.wait_y.wait_send()
 
 
 def scratch_shapes(nx, ny):
@@ -607,13 +682,13 @@
         for name in ("k", "b", "wx", "wy", "inv", "diag", "x", "s", "t"):
             shapes[name + str(i)] = pltpu.VMEM(lv.shape, F32)
         shapes["wz" + str(i)] = pltpu.VMEM((lv.parts + 1,) + lv.shape[1:], F32)
-        shapes["tmp" + str(i)] = pltpu.VMEM((max(lv.parts // 2, 1), lv.n // 2, max(lv.n, 8), LANES), F32)
+        shapes["tmp" + str(i)] = pltpu.VMEM((max(lv.parts // 2, 1), 8, 16, LANES), F32)
     shapes["e2"] = pltpu.VMEM((6, L2.rows, LANES), F32)
     for i, lv in ((3, l3), (4, l4), (5, l5)):
         for name in ("k", "b", "x", "s", "t"):
             shapes[name + str(i)] = pltpu.VMEM(lv.shape, F32)
         shapes["w" + str(i)] = pltpu.VMEM((8,) + lv.shape, F32)
-    for name, lv, halo in (("rk0", L0, 3), ("rb0", L0, 2), ("rs0", L0, 2), ("rk1", L1, 5), ("rb1", L1, 4)):
+    for name, lv, halo in (("rk0", L0, 3), ("rb0", L0, 2), ("rs0", L0, 2), ("rk1", L1, 7), ("rb1", L1, 6)):
         for j, shape in enumerate(Rim.scratch(lv, halo)):
             shapes[name + "_" + str(j)] = shape
     for name in ("rk2", "rb2", "rs2"):
@@ -621,10 +696,10 @@
             shapes[name + "_" + str(j)] = shape
     for name in ("pk3", "pb3"):
         shapes[name] = pltpu.VMEM((nx, 2, LANES), F32)
-    copies = 8 * 8 + 2 * (nx - 1 + ny - 1)
+    copies = 5 * 2 + 3 + 2 * 2
     shapes["send"] = pltpu.SemaphoreType.DMA((copies,))
     shapes["recv"] = pltpu.SemaphoreType.DMA((copies,))
-    shapes["local"] = pltpu.SemaphoreType.DMA((3,))
+    shapes["local"] = pltpu.SemaphoreType.DMA((4,))
     return shapes
 
 
@@ -648,7 +723,7 @@
         return cls(*args, refs)
 
     rk0, rb0, rs0 = (pair(name, Rim, L0, h) for name, h in (("rk0", 3), ("rb0", 2), ("rs0", 2)))
-    rk1, rb1 = (pair(name, Rim, L1, h) for name, h in (("rk1", 5), ("rb1", 4)))
+    rk1, rb1 = (pair(name, Rim, L1, h) for name, h in (("rk1", 7), ("rb1", 6)))
     rk2, rb2, rs2 = (pair(name, Blocks, L2) for name in ("rk2", "rb2", "rs2"))
     hk0, hb0, hs0, hk1, hb1, hk2, hb2, hs2 = (
         rim.exchange(place, links) for rim in (rk0, rb0, rs0, rk1, rb1, rk2, rb2, rs2)
@@ -662,22 +737,15 @@
     load_b.start()
 
     barrier = pltpu.get_barrier_semaphore()
-    for d in range(1, nx):
+    peers = [(dx, dy) for dx, dy in NEIGHBOURS]
+    peers += [(d, 0) for d in range(2, nx - 1)] + [(0, d) for d in range(2, ny - 1)]
+    for dx, dy in peers:
         pl.semaphore_signal(
-            barrier, inc=1, device_id=(lax.rem(gx + d, nx), gy), device_id_type=MESH
+            barrier,
+            inc=1,
+            device_id=(lax.rem(gx + dx + nx, nx), lax.rem(gy + dy + ny, ny)),
+            device_id_type=MESH,
         )
-    for d in range(1, ny):
-        pl.semaphore_signal(
-            barrier, inc=1, device_id=(gx, lax.rem(gy + d, ny)), device_id_type=MESH
-        )
-    corners = [d for d in NEIGHBOURS if d[0] and d[1]]
-    for dx, dy in corners:
-
-        @pl.when(there(place, dx, dy))
-        def _():
-            pl.semaphore_signal(
-                barrier, inc=1, device_id=(gx + dx, gy + dy), device_id_type=MESH
-            )
 
     def one(rows, cols, test):
         at = lax.broadcasted_iota(jnp.int32, (rows, cols), 0)
@@ -689,6 +757,9 @@
         m["perm"][pl.ds(start, 64), :] = one(
             64, 512, lambda at, to: at + start == 4 * (to % LANES) + to // LANES
         )
+
+    def fill_back(i):
+        start = pl.multiple_of(i * 64, 64)
         m["back"][pl.ds(start, 64), :] = one(
             64, 512, lambda at, to: to == 4 * ((at + start) % LANES) + (at + start) // LANES
         )
@@ -719,9 +790,7 @@
     load_k.wait()
     reorder(m["raw_k"], m["k0"])
     rk0.pack(m["k0"])
-    beside_x = jnp.where(gx > 0, 1, 0) + jnp.where(gx < nx - 1, 1, 0)
-    beside_y = jnp.where(gy > 0, 1, 0) + jnp.where(gy < ny - 1, 1, 0)
-    pl.semaphore_wait(barrier, nx - 1 + ny - 1 + beside_x * beside_y)
+    pl.semaphore_wait(barrier, len(peers))
     hk0.start()
     load_b.wait()
     reorder(m["raw_b"], m["b0"])
@@ -741,6 +810,7 @@
     for lv, i in ((l3, 3), (l4, 4), (l5, 5)):
         for name in ("k", "x", "s", "t"):
             zero_margin(lv, m[name + str(i)])
+    loop(8, 1, fill_back)
 
     weights = [
         tuple(m[name + str(i)] for name in ("wx", "wy", "wz", "inv", "diag")) for i in range(3)
@@ -766,24 +836,23 @@
     hk1.wait_recv()
     rk1.unpack(m["k1"], place)
     fine_setup(L1, m["k1"], weights[1], gx, gy, *sizes[1])
-    hb1.wait_recv()
-    rb1.unpack(m["b1"], place)
-    fine_first(L1, m["b1"], weights[1], m["x1"], 4)
-    fine_step(L1, m["b1"], weights[1], m["x1"], None, m["s1"], 3, KEEP, OLD, STEP)
-    fine_restrict(L1, m["b1"], weights[1], m["s1"], m["tmp1"])
-    fold_y(L1, m["tmp1"], m["b2"], L2.off, 0.5)
-    rb2.pack(m["b2"])
-    hb2.start()
-
     hk2.wait_recv()
     rk2.unpack(m["k2"], place)
     fine_setup(L2, m["k2"], weights[2], gx, gy, *sizes[2])
-    hb2.wait_recv()
-    rb2.unpack(m["b2"], place)
+
+    hb1.wait_recv()
+    rb1.unpack(m["b1"], place)
+    fine_first(L1, m["b1"], weights[1], m["x1"], 6)
+    fine_step(L1, m["b1"], weights[1], m["x1"], None, m["s1"], 5, KEEP, OLD, STEP)
+    fine_restrict(L1, m["b1"], weights[1], m["s1"], m["tmp1"], 4)
+    fold_y(L1, m["tmp1"], m["b2"], L2.off, 0.5, 4)
+
     fine_first(L2, m["b2"], weights[2], m["x2"], 2)
     fine_step(L2, m["b2"], weights[2], m["x2"], None, m["s2"], 1, KEEP, OLD, STEP)
     fine_restrict(L2, m["b2"], weights[2], m["s2"], m["tmp2"])
     gb3.start_x(fold_z(m["tmp2"], m["left"], fold, 0.5)[0:2])
+    rb2.pack(m["b2"])
+    hb2.start()
     rs2.pack(m["s2"])
     hs2.start()
 
@@ -794,6 +863,12 @@
     coarse_setup(l4, m["k4"], w4)
     coarse_fold(l4, l5, m["k4"], m["k5"], 0.125)
     coarse_setup(l5, m["k5"], w5)
+    for part in (hs0, hb2, hs2):
+        part.wait_recv()
+        part.wait_send()
+    rs0.unpack(m["s0"], place)
+    rb2.unpack(m["b2"], place)
+    rs2.unpack(m["s2"], place)
     gb3.finish()
 
     coarse_first(l3, m["b3"], w3, m["x3"])
@@ -833,9 +908,6 @@
                 m["e2"][i, pl.ds(ROW0 - 4 + 4 * d + 2 * a, 2), :] = jnp.broadcast_to(
                     row, (2, LANES)
                 )
-    hs2.wait_recv()
-    hs2.wait_send()
-    rs2.unpack(m["s2"], place)
     for i in range(6):
         for k in range(2):
             x = L2.off - 4 + 2 * i + k
@@ -850,14 +922,12 @@
     fine_step(L1, m["b1"], weights[1], m["t1"], None, m["x1"], 2, 1.0 - FIRST, 0.0, FIRST)
     fine_step(L1, m["b1"], weights[1], m["x1"], m["t1"], m["s1"], 1, KEEP, OLD, STEP)
 
-    hs0.wait_recv()
-    hs0.wait_send()
-    rs0.unpack(m["s0"], place)
     fine_correct(L0, L1, m["s1"], m["s0"], m["t0"], 2)
     fine_step(L0, m["b0"], weights[0], m["t0"], None, m["x0"], 1, 1.0 - FIRST, 0.0, FIRST)
     fine_step(L0, m["b0"], weights[0], m["x0"], m["t0"], m["s0"], 0, KEEP, OLD, STEP)
 
     half = L0.n // 2
+    stores = []
     for c in range(2):
         value = jnp.concatenate(
             [
@@ -870,11 +940,18 @@
         )
         moved = exact_dot(value, m["back"][...])
         m["out"][c * half : (c + 1) * half] = moved.reshape(half, L0.n, 512)
-    store = pltpu.make_async_copy(m["out"], out_ref, m["local"].at[2])
-    store.start()
-    for part in (hk0, hb0, hk1, hb1, hk2, hb2, gk3, gb3):
+        stores.append(
+            pltpu.make_async_copy(
+                m["out"].at[c * half : (c + 1) * half],
+                out_ref.at[c * half : (c + 1) * half],
+                m["local"].at[2 + c],
+            )
+        )
+        stores[c].start()
+    for part in (hk0, hb0, hk1, hb1, hk2, gk3, gb3):
         part.wait_send()
-    store.wait()
+    for store in stores:
+        store.wait()
 
 
 def solution(mesh):

time: 58.2 us -> 50.3 us (0.86)
  Pallas kernels: 56.1 us -> 48.3 us
    pallas_call x1, Pallas kernels: 56.1 us -> 48.3 us  [body(): pl.pallas_call(functools.partial(kernel, nx, ny, list(shapes)), out_shape...]
where the time goes in v2:
time: 50.3 us; the launch traced here: 50.2 us
  Pallas kernels  48.3 us (96%)
  local copies, waits for them, and re-layouts  1.88 us (4%)
    pallas_call x1, Pallas kernels, body(): pl.pallas_call(functools.partial(kernel, nx, ny, list(shapes)), out_shape...  48.3 us
    unnamed x1, local copies, waits for them, and re-layouts  1.88 us

profile of v2, /device:TPU:1, one launch (start us, length us, event | category | flops | bytes accessed | tf_op | source)
XLA Modules:
  0.0 50.2 jit_solution(7030341597993504113)
XLA Ops:
  0.0 48.3 %shard_map.28 = f32[16,16,512]{2,1,0:T(8,128)} custom-call(f32[16,16,512]{2,1,0:T(8,128)} %b_in.1, f32[16,16,512]{2,1,0:T(8,128)} %k_in.1), custom_call_target="tpu_custom_call" | custom-call | tf_op jit(solution)/shard_map/pallas_call | solution.py:962
  48.3 1.9 %copy.4 = f32[16,16,512]{2,1,0:T(8,128)} copy(f32[16,16,512]{2,1,0:T(8,128)} %shard_map.28) | data formatting | bytes 1048576

commit v3 on v2

--- a/solution.py
+++ b/solution.py
@@ -88,11 +88,17 @@
 
 
 def exact_dot(value, matrix):
-    total = None
-    for part in split3(value):
-        term = jnp.dot(part, matrix, preferred_element_type=F32)
-        total = term if total is None else total + term
-    return total
+    rows = value.shape[0]
+    moved = jnp.dot(
+        jnp.concatenate(split3(value), axis=0), matrix, preferred_element_type=F32
+    )
+    return (moved[:rows] + moved[rows : 2 * rows]) + moved[2 * rows :]
+
+
+def one(rows, cols, test):
+    at = lax.broadcasted_iota(jnp.int32, (rows, cols), 0)
+    to = lax.broadcasted_iota(jnp.int32, (rows, cols), 1)
+    return jnp.where(test(at, to), 1.0, 0.0).astype(BF16)
 
 
 class Batch:
@@ -120,12 +126,12 @@
     lane = lane_iota()
     row = lax.broadcasted_iota(jnp.int32, (8, LANES), 0)
     parts = lv.parts
-    count = lv.n + 2 * h + 1
+    start, count, tiles = -h, lv.n + 2 * h + 1, lv.tiles(h)
     width = turns(count, 12 // parts)
 
     def planes(i):
-        x = lv.off - h + width * i
-        for r in lv.tiles(h):
+        x = lv.off + start + width * i
+        for r in tiles:
             now = Batch()
             gy_cell = gy * lv.n + (r - ROW0) + row
             in_y = jnp.logical_and(gy_cell >= 0, gy_cell < size_y)
@@ -133,7 +139,7 @@
             below = [roll(c[parts - 1], 1) for c in cells]
             above = [roll(c[0], -1) for c in cells]
             for j in range(width):
-                gx_cell = gx * lv.n + (width * i + j - h)
+                gx_cell = gx * lv.n + (width * i + j + start)
                 inside = jnp.logical_and(in_y, jnp.logical_and(gx_cell >= 0, gx_cell < size_x))
                 first = jnp.where(lane == 0, 0.0, below[j])
                 last = jnp.where(lane == LANES - 1, 0.0, above[j])
@@ -200,13 +206,16 @@
     loop((lv.n + 2 * halo) // 2, 1, planes)
 
 
-def fine_step(lv, b_ref, w, v_ref, old_ref, out_ref, halo, keep, old, step):
+def fine_step(
+    lv, b_ref, w, v_ref, old_ref, out_ref, halo, keep, old, step, start=None, count=None
+):
     inv = w[3]
-    count = lv.n + 2 * halo
+    if count is None:
+        start, count = -halo, lv.n + 2 * halo
     width = turns(count, 8 // lv.parts)
 
     def planes(i):
-        x = lv.off - halo + width * i
+        x = lv.off + start + width * i
         for r in lv.tiles(halo):
             now = Batch()
             sums, cells = fine_sum(lv, now, v_ref, w, x, width, r)
@@ -335,7 +344,7 @@
 def coarse_setup(lv, k_ref, w):
     lane = lane_iota() % (LANES // 2)
     bottom, top = lane < lv.step, lane >= LANES // 2 - lv.step
-    group = 4 if lv.split else 8
+    group = 16 if lv.split else 8
 
     def planes(i):
         first = 1 + group * i
@@ -359,7 +368,7 @@
 
 
 def coarse_apply(lv, w, v_ref, out_ref, fn):
-    group = 4 if lv.split else 8
+    group = 16 if lv.split else 8
 
     def planes(i):
         first = 1 + group * i
@@ -526,18 +535,18 @@
 
 
 class Rim:
-    def __init__(self, lv, halo, refs):
-        self.lv, self.halo = lv, halo
+    def __init__(self, lv, halo, corner, refs):
+        self.lv, self.halo, self.corner = lv, halo, corner
         self.send_x, self.send_y, self.recv_x, self.recv_y = refs
 
     @staticmethod
-    def scratch(lv, halo):
+    def scratch(lv, halo, corner):
         n, parts = lv.n, lv.parts
         return [
             pltpu.VMEM((2, parts, halo, n, LANES), F32),
             pltpu.VMEM((2, parts, n, halo, LANES), F32),
             pltpu.VMEM((2, parts, halo, n, LANES), F32),
-            pltpu.VMEM((2, parts, n + 2 * halo, halo, LANES), F32),
+            pltpu.VMEM((2, parts, n + 2 * corner, halo, LANES), F32),
         ]
 
     def pack(self, ref):
@@ -555,7 +564,7 @@
         loop(lv.n, 2, plane)
 
     def exchange(self, place, links):
-        h, n = self.halo, self.lv.n
+        c, n = self.corner, self.lv.n
         faces, others = [], []
         for dx, dy in NEIGHBOURS:
             if dy == 0:
@@ -565,16 +574,16 @@
             src = self.send_y.at[1 if dy > 0 else 0]
             dst = self.recv_y.at[0 if dy > 0 else 1]
             if dx == 0:
-                dst = dst.at[:, h : h + n]
+                dst = dst.at[:, c : c + n]
             elif dx > 0:
-                src, dst = src.at[:, n - h : n], dst.at[:, 0:h]
+                src, dst = src.at[:, n - c : n], dst.at[:, 0:c]
             else:
-                src, dst = src.at[:, 0:h], dst.at[:, h + n : n + 2 * h]
+                src, dst = src.at[:, 0:c], dst.at[:, c + n : n + 2 * c]
             others.append(((dx, dy), src, dst))
         return Halo(place, links, [(others, self.recv_y), (faces, self.recv_x)])
 
     def unpack(self, ref, place):
-        lv, h, n = self.lv, self.halo, self.lv.n
+        lv, h, c, n = self.lv, self.halo, self.corner, self.lv.n
         for side, start, dx in ((0, lv.off - h, -1), (1, lv.off + n, 1)):
             ok = there(place, dx, 0)
             for p in range(lv.parts):
@@ -585,15 +594,15 @@
         gx, gy, nx, ny = place
 
         def plane(i):
-            cell = gx * n + (i - h)
+            cell = gx * n + (i - c)
             in_x = jnp.logical_and(cell >= 0, cell < nx * n)
             for side, row, dy in ((0, ROW0 - h, -1), (1, ROW0 + n, 1)):
                 ok = jnp.logical_and(in_x, there(place, 0, dy))
                 for p in range(lv.parts):
                     value = self.recv_y[side, p, i]
-                    ref[p, lv.off - h + i, pl.ds(row, h), :] = jnp.where(ok, value, 0.0)
-
-        loop(n + 2 * h, 2, plane)
+                    ref[p, lv.off - c + i, pl.ds(row, h), :] = jnp.where(ok, value, 0.0)
+
+        loop(n + 2 * c, 2, plane)
 
 
 class Blocks:
@@ -637,14 +646,16 @@
         gx, gy, nx, ny = place
         self.place = place
         self.piece, self.whole = piece_ref, whole_ref
+        order_x = sorted(range(1, nx), key=lambda d: -min(d // 2, (nx - d) // 2))
+        order_y = range(1, ny)
         mine = piece_ref.at[gx]
         copy = links.group()
-        self.along_x = [copy(mine, mine, (lax.rem(gx + d, nx), gy)) for d in range(1, nx)]
+        self.along_x = [copy(mine, mine, (lax.rem(gx + d, nx), gy)) for d in order_x]
         rest = piece_ref.at[0 : nx - 1]
         self.wait_x = copy(rest, rest, (lax.rem(gx + 1, nx), gy))
         slab = whole_ref.at[1 + gy, pl.ds(ROW0, 2 * nx), :]
         copy = links.group()
-        self.along_y = [copy(slab, slab, (gx, lax.rem(gy + d, ny))) for d in range(1, ny)]
+        self.along_y = [copy(slab, slab, (gx, lax.rem(gy + d, ny))) for d in order_y]
         rest = whole_ref.at[1:ny, pl.ds(ROW0, 2 * nx), :]
         self.wait_y = copy(rest, rest, (gx, lax.rem(gy + 1, ny)))
 
@@ -670,13 +681,21 @@
         self.wait_y.wait_send()
 
 
+RIMS = {
+    "rk0": (L0, 3, 2),
+    "rb0": (L0, 2, 1),
+    "rs0": (L0, 2, 1),
+    "rk1": (L1, 7, 7),
+    "rb1": (L1, 6, 5),
+}
+
+
 def scratch_shapes(nx, ny):
     l3, l4, l5 = coarse_levels(nx, ny)
     shapes = {}
-    for name in ("raw_k", "raw_b", "out"):
+    for name in ("raw_k", "raw_b"):
         shapes[name] = pltpu.VMEM((L0.n, L0.n, L0.parts * LANES), F32)
     shapes["perm"] = pltpu.VMEM((512, 512), BF16)
-    shapes["back"] = pltpu.VMEM((512, 512), BF16)
     shapes["left"] = pltpu.VMEM((8, 2 * LANES), F32)
     for i, lv in enumerate((L0, L1, L2)):
         for name in ("k", "b", "wx", "wy", "inv", "diag", "x", "s", "t"):
@@ -688,8 +707,8 @@
         for name in ("k", "b", "x", "s", "t"):
             shapes[name + str(i)] = pltpu.VMEM(lv.shape, F32)
         shapes["w" + str(i)] = pltpu.VMEM((8,) + lv.shape, F32)
-    for name, lv, halo in (("rk0", L0, 3), ("rb0", L0, 2), ("rs0", L0, 2), ("rk1", L1, 7), ("rb1", L1, 6)):
-        for j, shape in enumerate(Rim.scratch(lv, halo)):
+    for name, (lv, halo, corner) in RIMS.items():
+        for j, shape in enumerate(Rim.scratch(lv, halo, corner)):
             shapes[name + "_" + str(j)] = shape
     for name in ("rk2", "rb2", "rs2"):
         for j, shape in enumerate(Blocks.scratch(L2)):
@@ -722,8 +741,7 @@
         refs = [m[key] for key in names if key.startswith(name + "_")]
         return cls(*args, refs)
 
-    rk0, rb0, rs0 = (pair(name, Rim, L0, h) for name, h in (("rk0", 3), ("rb0", 2), ("rs0", 2)))
-    rk1, rb1 = (pair(name, Rim, L1, h) for name, h in (("rk1", 7), ("rb1", 6)))
+    rk0, rb0, rs0, rk1, rb1 = (pair(name, Rim, *RIMS[name]) for name in RIMS)
     rk2, rb2, rs2 = (pair(name, Blocks, L2) for name in ("rk2", "rb2", "rs2"))
     hk0, hb0, hs0, hk1, hb1, hk2, hb2, hs2 = (
         rim.exchange(place, links) for rim in (rk0, rb0, rs0, rk1, rb1, rk2, rb2, rs2)
@@ -747,21 +765,10 @@
             device_id_type=MESH,
         )
 
-    def one(rows, cols, test):
-        at = lax.broadcasted_iota(jnp.int32, (rows, cols), 0)
-        to = lax.broadcasted_iota(jnp.int32, (rows, cols), 1)
-        return jnp.where(test(at, to), 1.0, 0.0).astype(BF16)
-
     def fill(i):
         start = pl.multiple_of(i * 64, 64)
         m["perm"][pl.ds(start, 64), :] = one(
             64, 512, lambda at, to: at + start == 4 * (to % LANES) + to // LANES
-        )
-
-    def fill_back(i):
-        start = pl.multiple_of(i * 64, 64)
-        m["back"][pl.ds(start, 64), :] = one(
-            64, 512, lambda at, to: to == 4 * ((at + start) % LANES) + (at + start) // LANES
         )
 
     loop(8, 1, fill)
@@ -799,8 +806,6 @@
 
     fold_x(L0, m["k0"], m["tmp0"])
     fold_y(L0, m["tmp0"], m["k1"], L1.off, 0.125)
-    rk1.pack(m["k1"])
-    hk1.start()
     fold_x(L1, m["k1"], m["tmp1"])
     fold_y(L1, m["tmp1"], m["k2"], L2.off, 0.125)
     rk2.pack(m["k2"])
@@ -810,7 +815,6 @@
     for lv, i in ((l3, 3), (l4, 4), (l5, 5)):
         for name in ("k", "x", "s", "t"):
             zero_margin(lv, m[name + str(i)])
-    loop(8, 1, fill_back)
 
     weights = [
         tuple(m[name + str(i)] for name in ("wx", "wy", "wz", "inv", "diag")) for i in range(3)
@@ -819,6 +823,8 @@
     w3, w4, w5 = (m["w3"],), (m["w4"],), (m["w5"],)
 
     hk0.wait_recv()
+    rk1.pack(m["k1"])
+    hk1.start()
     rk0.unpack(m["k0"], place)
     fine_setup(L0, m["k0"], weights[0], gx, gy, *sizes[0])
     hb0.wait_recv()
@@ -924,26 +930,16 @@
 
     fine_correct(L0, L1, m["s1"], m["s0"], m["t0"], 2)
     fine_step(L0, m["b0"], weights[0], m["t0"], None, m["x0"], 1, 1.0 - FIRST, 0.0, FIRST)
-    fine_step(L0, m["b0"], weights[0], m["x0"], m["t0"], m["s0"], 0, KEEP, OLD, STEP)
-
     half = L0.n // 2
     stores = []
     for c in range(2):
-        value = jnp.concatenate(
-            [
-                m["s0"][p, pl.ds(L0.off + c * half, half), pl.ds(ROW0, L0.n), :].reshape(
-                    half * L0.n, LANES
-                )
-                for p in range(L0.parts)
-            ],
-            axis=1,
+        fine_step(
+            L0, m["b0"], weights[0], m["x0"], m["t0"], m["s0"], 0, KEEP, OLD, STEP, c * half, half
         )
-        moved = exact_dot(value, m["back"][...])
-        m["out"][c * half : (c + 1) * half] = moved.reshape(half, L0.n, 512)
         stores.append(
             pltpu.make_async_copy(
-                m["out"].at[c * half : (c + 1) * half],
-                out_ref.at[c * half : (c + 1) * half],
+                m["s0"].at[:, pl.ds(L0.off + c * half, half), pl.ds(ROW0, L0.n), :],
+                out_ref.at[:, pl.ds(c * half, half)],
                 m["local"].at[2 + c],
             )
         )
@@ -954,14 +950,53 @@
         store.wait()
 
 
+CHUNKS = 1
+
+
+def finish(parts_ref, out_ref, held, back, out, load_sem, store_sem):
+    n = L0.n
+    size = n // CHUNKS
+
+    def chunk(c):
+        return pl.ds(c * size, size)
+
+    loads = [
+        pltpu.make_async_copy(parts_ref.at[:, chunk(c)], held.at[:, chunk(c)], load_sem.at[c])
+        for c in range(CHUNKS)
+    ]
+    stores = [
+        pltpu.make_async_copy(out.at[chunk(c)], out_ref.at[chunk(c)], store_sem.at[c])
+        for c in range(CHUNKS)
+    ]
+    for load in loads:
+        load.start()
+
+    def fill(i):
+        start = pl.multiple_of(i * 64, 64)
+        back[pl.ds(start, 64), :] = one(
+            64, 512, lambda at, to: to == 4 * ((at + start) % LANES) + (at + start) // LANES
+        )
+
+    loop(8, 1, fill)
+    for c in range(CHUNKS):
+        loads[c].wait()
+        value = jnp.concatenate(
+            [held[p, chunk(c)].reshape(size * n, LANES) for p in range(L0.parts)], axis=1
+        )
+        out[chunk(c)] = exact_dot(value, back[...]).reshape(size, n, 512)
+        stores[c].start()
+    for store in stores:
+        store.wait()
+
+
 def solution(mesh):
     nx, ny = mesh.shape["gx"], mesh.shape["gy"]
     shapes = scratch_shapes(nx, ny)
 
     def body(right_side, coefficient):
-        return pl.pallas_call(
+        parts = pl.pallas_call(
             functools.partial(kernel, nx, ny, list(shapes)),
-            out_shape=jax.ShapeDtypeStruct(right_side.shape, F32),
+            out_shape=jax.ShapeDtypeStruct((L0.parts, L0.n, L0.n, LANES), F32),
             in_specs=[pl.BlockSpec(memory_space=pl.ANY)] * 2,
             out_specs=pl.BlockSpec(memory_space=pl.ANY),
             scratch_shapes=list(shapes.values()),
@@ -969,6 +1004,20 @@
                 collective_id=0, has_side_effects=True, vmem_limit_bytes=56 * 1024 * 1024
             ),
         )(right_side, coefficient)
+        return pl.pallas_call(
+            finish,
+            out_shape=jax.ShapeDtypeStruct(right_side.shape, F32),
+            in_specs=[pl.BlockSpec(memory_space=pl.ANY)],
+            out_specs=pl.BlockSpec(memory_space=pl.ANY),
+            scratch_shapes=[
+                pltpu.VMEM((L0.parts, L0.n, L0.n, LANES), F32),
+                pltpu.VMEM((512, 512), BF16),
+                pltpu.VMEM((L0.n, L0.n, 512), F32),
+                pltpu.SemaphoreType.DMA((CHUNKS,)),
+                pltpu.SemaphoreType.DMA((CHUNKS,)),
+            ],
+            compiler_params=pltpu.CompilerParams(vmem_limit_bytes=60 * 1024 * 1024),
+        )(parts)
 
     return jax.shard_map(
         body,

time: 50.3 us -> 47.3 us (0.940)
  local copies, waits for them, and re-layouts: 1.88 us -> 0 us
  Pallas kernels: 48.3 us -> 47.1 us
    pallas_call x1, Pallas kernels: 48.3 us -> 44.7 us  [body(): pl.pallas_call(functools.partial(kernel, nx, ny, list(shapes)), out_shape...]
    pallas_call x0 -> x1, Pallas kernels: none -> 2.43 us  [body(): pl.pallas_call(finish, out_shape=jax.ShapeDtypeStruct(right_side.shape, F...]
    unnamed x1 -> x0, local copies, waits for them, and re-layouts: 1.88 us -> none
where the time goes in v3:
time: 47.3 us; the launch traced here: 47.1 us
  Pallas kernels  47.1 us (100%)
    pallas_call x1, Pallas kernels, body(): pl.pallas_call(functools.partial(kernel, nx, ny, list(shapes)), out_shape...  44.7 us
    pallas_call x1, Pallas kernels, body(): pl.pallas_call(finish, out_shape=jax.ShapeDtypeStruct(right_side.shape, F...  2.43 us

profile of v3, /device:TPU:1, one launch (start us, length us, event | category | flops | bytes accessed | tf_op | source)
XLA Modules:
  0.0 47.1 jit_solution(17914950921690834282)
XLA Ops:
  0.0 44.7 %shard_map.28.parts_ref = f32[4,16,16,128]{3,2,1,0:T(8,128)} custom-call(f32[16,16,512]{2,1,0:T(8,128)} %b_in.1, f32[16,16,512]{2,1,0:T(8,128)} %k_in.1), custom_call_target="tpu_custom_call" | custom-call | tf_op jit(solution)/shard_map/pallas_call | solution.py:997
  44.7 2.4 %shard_map.29 = f32[16,16,512]{2,1,0:T(8,128)} custom-call(f32[4,16,16,128]{3,2,1,0:T(8,128)} %shard_map.28.parts_ref), custom_call_target="tpu_custom_call" | custom-call | tf_op jit(solution)/shard_map/pallas_call | solution.py:1007

commit v4 on v3

--- a/solution.py
+++ b/solution.py
@@ -212,7 +212,7 @@
     inv = w[3]
     if count is None:
         start, count = -halo, lv.n + 2 * halo
-    width = turns(count, 8 // lv.parts)
+    width = turns(count, 16 // lv.parts)
 
     def planes(i):
         x = lv.off + start + width * i
@@ -344,7 +344,7 @@
 def coarse_setup(lv, k_ref, w):
     lane = lane_iota() % (LANES // 2)
     bottom, top = lane < lv.step, lane >= LANES // 2 - lv.step
-    group = 16 if lv.split else 8
+    group = lv.planes
 
     def planes(i):
         first = 1 + group * i
@@ -368,7 +368,7 @@
 
 
 def coarse_apply(lv, w, v_ref, out_ref, fn):
-    group = 16 if lv.split else 8
+    group = lv.planes
 
     def planes(i):
         first = 1 + group * i
@@ -463,7 +463,7 @@
             for at, value in held:
                 t_ref[at] = value
 
-    loop(next_lv.planes, 4, plane)
+    loop(next_lv.planes, 8, plane)
 
 
 def zero_margin(lv, ref):
@@ -685,7 +685,7 @@
     "rk0": (L0, 3, 2),
     "rb0": (L0, 2, 1),
     "rs0": (L0, 2, 1),
-    "rk1": (L1, 7, 7),
+    "rk1": (L1, 7, 6),
     "rb1": (L1, 6, 5),
 }
 

time: 47.3 us -> 46.3 us (0.979)
  Pallas kernels: 47.1 us -> 46.2 us
    pallas_call x1, Pallas kernels: 44.7 us -> 43.8 us  [body(): pl.pallas_call(functools.partial(kernel, nx, ny, list(shapes)), out_shape...]
where the time goes in v4:
time: 46.3 us; the launch traced here: 46.2 us
  Pallas kernels  46.2 us (100%)
    pallas_call x1, Pallas kernels, body(): pl.pallas_call(functools.partial(kernel, nx, ny, list(shapes)), out_shape...  43.8 us
    pallas_call x1, Pallas kernels, body(): pl.pallas_call(finish, out_shape=jax.ShapeDtypeStruct(right_side.shape, F...  2.42 us

profile of v4, /device:TPU:1, one launch (start us, length us, event | category | flops | bytes accessed | tf_op | source)
XLA Modules:
  0.0 46.2 jit_solution(18298406345846186811)
XLA Ops:
  0.0 43.8 %shard_map.28.parts_ref = f32[4,16,16,128]{3,2,1,0:T(8,128)} custom-call(f32[16,16,512]{2,1,0:T(8,128)} %b_in.1, f32[16,16,512]{2,1,0:T(8,128)} %k_in.1), custom_call_target="tpu_custom_call" | custom-call | tf_op jit(solution)/shard_map/pallas_call | solution.py:997
  43.8 2.4 %shard_map.29 = f32[16,16,512]{2,1,0:T(8,128)} custom-call(f32[4,16,16,128]{3,2,1,0:T(8,128)} %shard_map.28.parts_ref), custom_call_target="tpu_custom_call" | custom-call | tf_op jit(solution)/shard_map/pallas_call | solution.py:1007
